TPU v7x, 32 devices: a whole 2x2x4 slice. The times are simulated.
32 devices in a mesh: dp: 8 (over y, x, core), fsdp: 4 (over z).
Axes of the slice: x: 2, y: 2, z: 4, core: 2. Of those that a mesh axis runs over, the one named last changes fastest.
Arguments:
- token_ids: int32 [64, 512], P(('dp', 'fsdp')), may hold values from 0 to 50303
- true_mask: int32 [64, 512], P(('dp', 'fsdp')), may hold values from 0 to 1, as said below
- keep_layer: int32 [64], P(('dp', 'fsdp')), may hold values 0 or 1
- picked: int32 [64, 64], P(('dp', 'fsdp')), may hold values from 0 to 511, as said below
- teacher_hidden: bfloat16 [64, 512, 768], P(('dp', 'fsdp')), may hold values from -8 to 8
- teacher_logits: bfloat16 [64, 64, 50304], P(('dp', 'fsdp')), may hold values from -12 to 12
- embed_table: float32 [50304, 768], P(('dp', 'fsdp'))
- pos_table: float32 [512, 768], P(None, ('dp', 'fsdp')), may hold values from -0.21875 to 0.21875
- query_key_value_weight: float32 [768, 2304], P(('dp', 'fsdp')), may hold values from -0.21875 to 0.21875
- output_weight: float32 [768, 768], P(('dp', 'fsdp')), may hold values from -0.875 to 0.875
- up_weight: float32 [768, 3072], P(('dp', 'fsdp')), may hold values from -0.21875 to 0.21875
- down_weight: float32 [3072, 768], P(('dp', 'fsdp')), may hold values from -0.109375 to 0.109375
- gains_biases: float32 [14, 768], P(None, ('dp', 'fsdp'))
- first_embed: float32 [50304, 768], P(('dp', 'fsdp')), may hold values from -4.5776367e-05 to 4.5776367e-05
- first_pos: float32 [512, 768], P(None, ('dp', 'fsdp')), may hold values from -4.5776367e-05 to 4.5776367e-05
- first_qkv: float32 [768, 2304], P(('dp', 'fsdp')), may hold values from -4.5776367e-05 to 4.5776367e-05
- first_out: float32 [768, 768], P(('dp', 'fsdp')), may hold values from -4.5776367e-05 to 4.5776367e-05
- first_up: float32 [768, 3072], P(('dp', 'fsdp')), may hold values from -4.5776367e-05 to 4.5776367e-05
- first_down: float32 [3072, 768], P(('dp', 'fsdp')), may hold values from -4.5776367e-05 to 4.5776367e-05
- first_gains: float32 [14, 768], P(None, ('dp', 'fsdp')), may hold values from -0.00018310547 to 0.00018310547
- second_embed: float32 [50304, 768], P(('dp', 'fsdp')), may hold values from 5.421191e-12 to 2.1684763e-11
- second_pos: float32 [512, 768], P(None, ('dp', 'fsdp')), may hold values from 5.421191e-12 to 2.1684763e-11
- second_qkv: float32 [768, 2304], P(('dp', 'fsdp')), may hold values from 5.421191e-12 to 2.1684763e-11
- second_out: float32 [768, 768], P(('dp', 'fsdp')), may hold values from 5.421191e-12 to 2.1684763e-11
- second_up: float32 [768, 3072], P(('dp', 'fsdp')), may hold values from 5.421191e-12 to 2.1684763e-11
- second_down: float32 [3072, 768], P(('dp', 'fsdp')), may hold values from 5.421191e-12 to 2.1684763e-11
- second_gains: float32 [14, 768], P(None, ('dp', 'fsdp')), may hold values from 8.673905e-11 to 3.469562e-10
Outputs:
- loss_sum: float32 [], replicated
- token_count: float32 [], replicated
- grad_norm: float32 [], replicated
- new_embed: float32 [50304, 768], P(('dp', 'fsdp'))
- new_pos: float32 [512, 768], P(None, ('dp', 'fsdp'))
- new_qkv: float32 [768, 2304], P(('dp', 'fsdp'))
- new_out: float32 [768, 768], P(('dp', 'fsdp'))
- new_up: float32 [768, 3072], P(('dp', 'fsdp'))
- new_down: float32 [3072, 768], P(('dp', 'fsdp'))
- new_gains: float32 [14, 768], P(None, ('dp', 'fsdp'))
- moment_embed: float32 [50304, 768], P(('dp', 'fsdp'))
- moment_pos: float32 [512, 768], P(None, ('dp', 'fsdp'))
- moment_qkv: float32 [768, 2304], P(('dp', 'fsdp'))
- moment_out: float32 [768, 768], P(('dp', 'fsdp'))
- moment_up: float32 [768, 3072], P(('dp', 'fsdp'))
- moment_down: float32 [3072, 768], P(('dp', 'fsdp'))
- moment_gains: float32 [14, 768], P(None, ('dp', 'fsdp'))
- square_embed: float32 [50304, 768], P(('dp', 'fsdp'))
- square_pos: float32 [512, 768], P(None, ('dp', 'fsdp'))
- square_qkv: float32 [768, 2304], P(('dp', 'fsdp'))
- square_out: float32 [768, 768], P(('dp', 'fsdp'))
- square_up: float32 [768, 3072], P(('dp', 'fsdp'))
- square_down: float32 [3072, 768], P(('dp', 'fsdp'))
- square_gains: float32 [14, 768], P(None, ('dp', 'fsdp'))
- matrix_norms: float32 [2, 7], replicated
Inputs may be any that keep to these rules, and one draw needn't show every extreme that they name: `true_mask`: in each sequence the true tokens are the first ones, at least one. `picked`: each entry is a position of a true token of its sequence.
All inputs are finite; a program needn't handle non-finite values. No bound on the sum of `keep_layer` on one device may be relied on, other than what follows from the above.
Results may differ from a plain program's by a relative error of at most 0.0098.
The roundings to bfloat16 on the way count: a program that leaves them out, or rounds other values in their place, can miss the bound.
Values may be sent and summed in bfloat16 or wider, within the bound.
No kernel may reach another device: no remote copies, remote signals or barrier semaphores. Data moves between devices by JAX's collectives and lax.ppermute only.
A program may use at most 832 MiB of HBM per device.

v0:
```python
import jax
import jax.numpy as jnp
from jax import lax
from jax.sharding import PartitionSpec as P

H = 12
HD = 64
STEP = 10


NORM_EPS = 1e-05
CLIP_NORM = 0.5
BETA_ONE = 0.9
BETA_TWO = 0.999
ADAM_EPS = 1e-06
DECAY_RATE = 0.01
LEARN_RATE = 0.3
MASKED_SCORE = -1e30


def norm_rows(values, gain_row, shift_row):
    row_mean = jnp.mean(values, axis=-1, keepdims=True)
    centered = values - row_mean
    row_var = jnp.mean(centered * centered, axis=-1, keepdims=True)
    return centered * lax.rsqrt(row_var + NORM_EPS) * gain_row + shift_row


def gelu_exact(values):
    return jax.nn.gelu(values, approximate=False)


def dense(left_op, right_op):
    return jnp.dot(left_op, right_op, preferred_element_type=jnp.float32)


def dense_tn(left_op, right_op):
    return lax.dot_general(
        left_op, right_op, (((0,), (0,)), ((), ())), preferred_element_type=jnp.float32
    )


def dense_nt(left_op, right_op):
    return lax.dot_general(
        left_op, right_op, (((1,), (1,)), ((), ())), preferred_element_type=jnp.float32
    )


def scores_of(queries, key_rows, key_live):
    raw_scores = jnp.einsum(
        "sqhe,skhe->shqk", queries, key_rows, preferred_element_type=jnp.float32
    ) * HD ** (-0.5)
    return jnp.where(key_live[:, None, None, :], raw_scores, MASKED_SCORE)


def split_heads(packed, seq_count):
    shaped = packed.reshape(seq_count, -1, 3, H, HD)
    return (shaped[:, :, 0], shaped[:, :, 1], shaped[:, :, 2])


def layer_forward(layer_inputs, key_live, matrices, vector_params):
    qkv_low, out_low, up_low, down_low = matrices
    seq_count = layer_inputs.shape[0]
    row_width = layer_inputs.shape[2]
    flat_in = layer_inputs.reshape(-1, row_width)
    flat_low = flat_in.astype(jnp.bfloat16)
    qkv_bias = jnp.concatenate(
        [vector_params[2], jnp.zeros_like(vector_params[2]), vector_params[3]]
    )
    packed = (dense(flat_low, qkv_low) + qkv_bias).astype(jnp.bfloat16)
    queries, key_rows, values = split_heads(packed, seq_count)
    scores = scores_of(queries, key_rows, key_live)
    score_peak = jnp.max(scores, axis=-1, keepdims=True)
    exponent = jnp.exp(scores - score_peak)
    exp_total = jnp.sum(exponent, axis=-1, keepdims=True)
    softmaxed = (exponent / exp_total).astype(jnp.bfloat16)
    log_total = score_peak + jnp.log(exp_total)
    mixed_output = jnp.einsum(
        "shqk,skhe->sqhe", softmaxed, values, preferred_element_type=jnp.float32
    )
    mixed_output = mixed_output.reshape(-1, row_width).astype(jnp.bfloat16)
    joined_one = flat_in + (dense(mixed_output, out_low) + vector_params[4])
    first_normed = norm_rows(joined_one, vector_params[5], vector_params[6])
    normed_low = first_normed.astype(jnp.bfloat16)
    hidden_state = dense(normed_low, up_low) + vector_params[10:14].reshape(-1)
    gelu_activated = gelu_exact(hidden_state).astype(jnp.bfloat16)
    joined_two = first_normed + (dense(gelu_activated, down_low) + vector_params[7])
    result = norm_rows(joined_two, vector_params[8], vector_params[9]).reshape(layer_inputs.shape)
    saved_state = (
        flat_low,
        packed,
        log_total,
        mixed_output,
        joined_one,
        normed_low,
        hidden_state,
        gelu_activated,
        joined_two,
    )
    return (result, saved_state)


def layer_backward(grad_out, key_live, matrices, vector_params, saved_state):
    qkv_low, out_low, up_low, down_low = matrices
    (
        flat_low,
        packed,
        log_total,
        mixed_output,
        joined_one,
        normed_low,
        hidden_state,
        gelu_activated,
        joined_two,
    ) = saved_state
    seq_count = key_live.shape[0]
    row_width = flat_low.shape[1]
    scale_factor = HD ** (-0.5)
    _, back_two = jax.vjp(norm_rows, joined_two, vector_params[8], vector_params[9])
    grad_joined_two, gain_two, shift_two = back_two(grad_out)
    grad_feed = grad_joined_two.astype(jnp.bfloat16)
    _, back_gelu = jax.vjp(gelu_exact, hidden_state)
    grad_hidden = back_gelu(dense_nt(grad_feed, down_low))[0].astype(jnp.bfloat16)
    grad_normed = grad_joined_two + dense_nt(grad_hidden, up_low)
    _, back_one = jax.vjp(norm_rows, joined_one, vector_params[5], vector_params[6])
    grad_joined_one, gain_one, shift_one = back_one(grad_normed)
    grad_attention = grad_joined_one.astype(jnp.bfloat16)
    grad_mixed = (
        dense_nt(grad_attention, out_low).astype(jnp.bfloat16).reshape(seq_count, -1, H, HD)
    )
    queries, key_rows, values = split_heads(packed, seq_count)
    softmaxed = jnp.exp(scores_of(queries, key_rows, key_live) - log_total)
    grad_values = jnp.einsum(
        "shqk,sqhe->skhe",
        softmaxed.astype(jnp.bfloat16),
        grad_mixed,
        preferred_element_type=jnp.float32,
    )
    grad_weights = jnp.einsum(
        "sqhe,skhe->shqk", grad_mixed, values, preferred_element_type=jnp.float32
    )
    grad_scores = softmaxed * (
        grad_weights - jnp.sum(grad_weights * softmaxed, axis=-1, keepdims=True)
    )
    grad_scores = grad_scores.astype(jnp.bfloat16)
    grad_queries = (
        jnp.einsum("shqk,skhe->sqhe", grad_scores, key_rows, preferred_element_type=jnp.float32)
        * scale_factor
    )
    grad_keys = (
        jnp.einsum("shqk,sqhe->skhe", grad_scores, queries, preferred_element_type=jnp.float32)
        * scale_factor
    )
    grad_packed = (
        jnp.stack([grad_queries, grad_keys, grad_values], axis=2)
        .reshape(-1, 3 * row_width)
        .astype(jnp.bfloat16)
    )
    grad_inputs = grad_joined_one + dense_nt(grad_packed, qkv_low)
    matrix_grads = (
        dense_tn(flat_low, grad_packed),
        dense_tn(mixed_output, grad_attention),
        dense_tn(normed_low, grad_hidden),
        dense_tn(gelu_activated, grad_feed),
    )
    packed_sum = jnp.sum(grad_packed, axis=0, dtype=jnp.float32)
    vector_rows = jnp.stack(
        [
            packed_sum[:row_width],
            packed_sum[2 * row_width :],
            jnp.sum(grad_attention, axis=0, dtype=jnp.float32),
            gain_one,
            shift_one,
            jnp.sum(grad_feed, axis=0, dtype=jnp.float32),
            gain_two,
            shift_two,
        ]
    )
    up_rows = jnp.sum(grad_hidden, axis=0, dtype=jnp.float32).reshape(4, row_width)
    return (grad_inputs, matrix_grads, jnp.concatenate([vector_rows, up_rows]))


def on_device(
    token_ids,
    true_mask,
    keep_layer,
    picked,
    teacher_hidden,
    teacher_logits,
    embed_table,
    pos_table,
    query_key_value_weight,
    output_weight,
    up_weight,
    down_weight,
    gains_biases,
    first_embed,
    first_pos,
    first_qkv,
    first_out,
    first_up,
    first_down,
    first_gains,
    second_embed,
    second_pos,
    second_qkv,
    second_out,
    second_up,
    second_down,
    second_gains,
):
    masters = (
        embed_table,
        pos_table,
        query_key_value_weight,
        output_weight,
        up_weight,
        down_weight,
        gains_biases,
    )
    firsts = (first_embed, first_pos, first_qkv, first_out, first_up, first_down, first_gains)
    seconds = (
        second_embed,
        second_pos,
        second_qkv,
        second_out,
        second_up,
        second_down,
        second_gains,
    )
    lowered = tuple((weight.astype(jnp.bfloat16) for weight in masters))
    gathered = (
        lax.all_gather(lowered[0], ("dp", "fsdp"), axis=0, tiled=True),
        lax.all_gather(lowered[1], ("dp", "fsdp"), axis=1, tiled=True),
        lax.all_gather(lowered[2], ("dp", "fsdp"), axis=0, tiled=True),
        lax.all_gather(lowered[3], ("dp", "fsdp"), axis=0, tiled=True),
        lax.all_gather(lowered[4], ("dp", "fsdp"), axis=0, tiled=True),
        lax.all_gather(lowered[5], ("dp", "fsdp"), axis=0, tiled=True),
        lax.all_gather(lowered[6], ("dp", "fsdp"), axis=1, tiled=True),
    )
    embed_full, pos_full, qkv_full, out_full, up_full, down_full, vector_full = gathered
    vector_params = vector_full.astype(jnp.float32)
    matrices = (qkv_full, out_full, up_full, down_full)
    seq_count = token_ids.shape[0]
    row_width = embed_table.shape[1]
    embedded = (
        jnp.take(embed_full, token_ids, axis=0).astype(jnp.float32)
        + pos_full.astype(jnp.float32)[None]
    )
    layer_inputs = norm_rows(embedded, vector_params[0], vector_params[1])
    key_live = true_mask > 0
    layer_out, saved_state = layer_forward(layer_inputs, key_live, matrices, vector_params)
    keep_rows = (keep_layer > 0)[:, None, None]
    final_rows = jnp.where(keep_rows, layer_out, layer_inputs)
    weighted = true_mask.astype(jnp.float32)[:, :, None]
    hidden_gap = final_rows - teacher_hidden.astype(jnp.float32)
    loss_part = jnp.sum(weighted * hidden_gap * hidden_gap)
    grad_final = 2.0 * weighted * hidden_gap
    chosen = (
        jnp.take_along_axis(final_rows, picked[:, :, None], axis=1)
        .reshape(-1, row_width)
        .astype(jnp.bfloat16)
    )
    all_chosen = lax.all_gather(chosen, ("dp", "fsdp"), axis=0, tiled=True)
    target_cols = lax.all_to_all(
        teacher_logits, ("dp", "fsdp"), split_axis=2, concat_axis=0, tiled=True
    )
    logits = dense_nt(all_chosen, lowered[0])
    mismatch = logits - target_cols.reshape(logits.shape).astype(jnp.float32)
    grad_logits = (2.0 * mismatch).astype(jnp.bfloat16)
    head_local = dense_tn(grad_logits, all_chosen)
    grad_chosen = lax.psum_scatter(
        dense(grad_logits, lowered[0]), ("dp", "fsdp"), scatter_dimension=0, tiled=True
    )
    loss_part = loss_part + jnp.sum(mismatch * mismatch)
    seq_index = jnp.arange(seq_count)[:, None]
    grad_final = grad_final.at[seq_index, picked].add(grad_chosen.reshape(seq_count, -1, row_width))
    grad_layer = jnp.where(keep_rows, grad_final, 0.0)
    grad_inputs, matrix_grads, vector_grads = layer_backward(
        grad_layer.reshape(-1, row_width), key_live, matrices, vector_params, saved_state
    )
    grad_inputs = jnp.where(keep_rows, 0.0, grad_final) + grad_inputs.reshape(grad_final.shape)
    _, back_zero = jax.vjp(norm_rows, embedded, vector_params[0], vector_params[1])
    grad_embedded, gain_zero, shift_zero = back_zero(grad_inputs)
    grad_pos = jnp.sum(grad_embedded, axis=0)
    flat_ids = token_ids.reshape(-1)
    flat_grad = grad_embedded.reshape(-1, row_width)
    count_rows = embed_table.shape[0] * lax.axis_size(("dp", "fsdp"))
    inside = (flat_ids >= 0) & (flat_ids < count_rows)
    slot_ids = jnp.where(inside, flat_ids, count_rows)
    term_rows = jax.ops.segment_sum(flat_grad, slot_ids, num_segments=count_rows + 1)[:count_rows]
    table_grad = lax.psum_scatter(term_rows, ("dp", "fsdp"), scatter_dimension=0, tiled=True)
    table_grad = table_grad + head_local
    vector_all = jnp.concatenate([jnp.stack([gain_zero, shift_zero]), vector_grads])
    reduced = (
        lax.psum_scatter(grad_pos, ("dp", "fsdp"), scatter_dimension=1, tiled=True),
        lax.psum_scatter(matrix_grads[0], ("dp", "fsdp"), scatter_dimension=0, tiled=True),
        lax.psum_scatter(matrix_grads[1], ("dp", "fsdp"), scatter_dimension=0, tiled=True),
        lax.psum_scatter(matrix_grads[2], ("dp", "fsdp"), scatter_dimension=0, tiled=True),
        lax.psum_scatter(matrix_grads[3], ("dp", "fsdp"), scatter_dimension=0, tiled=True),
        lax.psum_scatter(vector_all, ("dp", "fsdp"), scatter_dimension=1, tiled=True),
    )
    gradients = (table_grad,) + tuple(reduced)
    grad_squares = jnp.stack([jnp.sum(member * member) for member in gradients])
    weight_squares = jnp.stack([jnp.sum(member * member) for member in masters])
    loss_sum, token_count, grad_squares, weight_squares = lax.psum(
        (loss_part, jnp.sum(weighted), grad_squares, weight_squares), ("dp", "fsdp")
    )
    grad_norm = jnp.sqrt(jnp.sum(grad_squares)) / token_count
    factor = jnp.minimum(1.0, CLIP_NORM / grad_norm) / token_count
    updates = []
    new_moments = []
    new_squares = []
    for weight, gradient, moment, square in zip(masters, gradients, firsts, seconds):
        clipped = gradient * factor
        moment_new = BETA_ONE * moment + (1.0 - BETA_ONE) * clipped
        square_new = BETA_TWO * square + (1.0 - BETA_TWO) * clipped * clipped
        updates.append(
            moment_new
            / (1.0 - BETA_ONE**STEP)
            / (jnp.sqrt(square_new / (1.0 - BETA_TWO**STEP)) + ADAM_EPS)
            + DECAY_RATE * weight
        )
        new_moments.append(moment_new)
        new_squares.append(square_new)
    update_squares = lax.psum(
        jnp.stack([jnp.sum(update * update) for update in updates]), ("dp", "fsdp")
    )
    weight_norms = jnp.sqrt(weight_squares)
    update_norms = jnp.sqrt(update_squares)
    ratios = weight_norms / update_norms
    new_weights = [
        weight - LEARN_RATE * ratios[position] * update
        for position, (weight, update) in enumerate(zip(masters, updates))
    ]
    matrix_norms = jnp.stack([weight_norms, update_norms])
    return (
        loss_sum,
        token_count,
        grad_norm,
        new_weights[0],
        new_weights[1],
        new_weights[2],
        new_weights[3],
        new_weights[4],
        new_weights[5],
        new_weights[6],
        new_moments[0],
        new_moments[1],
        new_moments[2],
        new_moments[3],
        new_moments[4],
        new_moments[5],
        new_moments[6],
        new_squares[0],
        new_squares[1],
        new_squares[2],
        new_squares[3],
        new_squares[4],
        new_squares[5],
        new_squares[6],
        matrix_norms,
    )


def solution(mesh):
    placed = (
        P(("dp", "fsdp"), None),
        P(("dp", "fsdp"), None),
        P(("dp", "fsdp")),
        P(("dp", "fsdp"), None),
        P(("dp", "fsdp"), None, None),
        P(("dp", "fsdp"), None, None),
        P(("dp", "fsdp"), None),
        P(None, ("dp", "fsdp")),
        P(("dp", "fsdp"), None),
        P(("dp", "fsdp"), None),
        P(("dp", "fsdp"), None),
        P(("dp", "fsdp"), None),
        P(None, ("dp", "fsdp")),
        P(("dp", "fsdp"), None),
        P(None, ("dp", "fsdp")),
        P(("dp", "fsdp"), None),
        P(("dp", "fsdp"), None),
        P(("dp", "fsdp"), None),
        P(("dp", "fsdp"), None),
        P(None, ("dp", "fsdp")),
        P(("dp", "fsdp"), None),
        P(None, ("dp", "fsdp")),
        P(("dp", "fsdp"), None),
        P(("dp", "fsdp"), None),
        P(("dp", "fsdp"), None),
        P(("dp", "fsdp"), None),
        P(None, ("dp", "fsdp")),
    )
    return jax.shard_map(
        on_device,
        mesh=mesh,
        in_specs=placed,
        out_specs=(
            P(),
            P(),
            P(),
            P(("dp", "fsdp"), None),
            P(None, ("dp", "fsdp")),
            P(("dp", "fsdp"), None),
            P(("dp", "fsdp"), None),
            P(("dp", "fsdp"), None),
            P(("dp", "fsdp"), None),
            P(None, ("dp", "fsdp")),
            P(("dp", "fsdp"), None),
            P(None, ("dp", "fsdp")),
            P(("dp", "fsdp"), None),
            P(("dp", "fsdp"), None),
            P(("dp", "fsdp"), None),
            P(("dp", "fsdp"), None),
            P(None, ("dp", "fsdp")),
            P(("dp", "fsdp"), None),
            P(None, ("dp", "fsdp")),
            P(("dp", "fsdp"), None),
            P(("dp", "fsdp"), None),
            P(("dp", "fsdp"), None),
            P(("dp", "fsdp"), None),
            P(None, ("dp", "fsdp")),
            P(),
        ),
        check_vma=False,
    )
```

profile of v0, /device:TPU:0, one launch (start us, length us, event | category | flops | bytes accessed | tf_op | source)
XLA Modules:
  0.0 5476.6 jit_solution(9868309861530987286)
XLA Ops:
  13.7 52.0 copy.139
  65.6 36.7 reshape.489
  102.4 7.3 all-to-all-start
  112.4 612.9 %all-gather.1 = bf16[32,24,14]{1,2,0:T(8,128)(2,1)S(1)} all-gather(bf16[1,24,14]{1,2,0:T(8,128)(2,1)S(1)} %convert_bitcast_fusion), channel_id=1, replica_groups=mesh['dp'=8,'fsdp'=4] {'dp','fsdp'}, dimensions={0}, use_global_device_ids=true | all-gather | bytes 22176 | tf_op jit(solution)/shard_map/all_gather | solution.py:238
  728.1 73.5 %all_gather.25 = bf16[512,768]{0,1:T(8,128)(2,1)S(1)} all-gather(bf16[512,24]{0,1:T(8,128)(2,1)S(1)} %convert_element_type.147), channel_id=1, replica_groups=mesh['dp'=8,'fsdp'=4] {'dp','fsdp'}, dimensions={1}, use_global_device_ids=true | all-gather | bytes 811008 | tf_op jit(solution)/shard_map/all_gather | solution.py:233
  801.9 89.0 %reshape.471 = bf16[50304,768]{1,0:T(8,128)(2,1)} reshape(bf16[32,1572,768]{2,1,0:T(8,128)(2,1)} %all-gather.19.cloned.1.call-done) | data formatting | bytes 154533888
  890.9 13.8 gather_fusion
  909.1 8.5 add_convert_fusion.1
  917.6 6.6 copy.133
  924.2 8.8 reshape.422
  933.1 5.0 fusion.80
  938.1 11.2 fusion.13
  949.3 11.6 fusion.1
  961.0 11.4 fusion.35
  982.0 38.2 multiply_convert_fusion.2
  1020.1 9.3 fusion.84
  1039.5 37.9 reshape.490
  1077.4 61.9 %copy.140 = f32[2,64,32,1572]{3,1,0,2:T(8,128)} copy(bf16[2,64,32,1572]{1,0,3,2:T(2,128)(2,1)} %bitcast.190) | data formatting | bytes 38633472 | tf_op jit(solution)/shard_map/convert_element_type | solution.py:268
  1139.3 28.1 copy.141
  1167.5 27.2 multiply_reduce_fusion
  1194.7 21.0 fusion.15
  1216.6 152.0 %reduce-scatter.12.cloned.1.call-done = f32[128,768]{1,0:T(8,128)} async-done(((f32[4096,768]{1,0:T(8,128)}), f32[128,768]{1,0:T(8,128)}) %reduce-scatter.12.cloned.1.call-update) | async-done | bytes 393232 | tf_op jit(solution)/shard_map/reduce_scatter | solution.py:271
  1368.6 12.4 scatter_fusion
  1389.3 18.9 convert_reduce_fusion
  1408.2 10.2 multiply_reduce_fusion.5
  1433.1 12.4 fusion.31
  1445.5 20.0 multiply_reduce_fusion.1
  1465.4 21.7 multiply_convert_fusion.1
  1487.1 8.6 multiply_bitcast_fusion
  1495.7 6.8 multiply_bitcast_fusion.1
  1505.9 9.4 copy.148
  1539.1 4.9 fusion.86
  1544.0 9.7 fusion.85
  1554.5 10.7 fusion.63
  1565.8 48.7 broadcast_in_dim.139
  1614.6 131.2 %scatter_fusion.1 = f32[50305,768]{1,0:T(8,128)} fusion(f32[50305,768]{1,0:T(8,128)} %broadcast_in_dim.139, s32[1024]{0:T(1024)S(1)} %bitcast.213, f32[1024,768]{1,0:T(8,128)S(1)} %bitcast.192), kind=kCustom, calls=%fused_computation.3 | custom fusion | flops 786432 | bytes 9441280 | tf_op jit(solution)/shard_map/scatter-add | solution.py:290
  1745.8 103.4 %slice.124 = f32[50304,768]{1,0:T(8,128)} slice(f32[50305,768]{1,0:T(8,128)} %scatter_fusion.1), slice={[0:50304], [0:768]} | slice | bytes 309067776 | tf_op jit(solution)/shard_map/slice | solution.py:290
  1849.2 10.1 fusion.87
  1859.4 3372.4 %fusion = f32[1584,768]{1,0:T(8,128)} fusion(f32[50304,768]{1,0:T(8,128)} %slice.124), kind=kCustom, calls=%all-reduce-scatter | all-reduce-scatter fusion | flops 38928384 | bytes 159399936
  5234.3 5.4 collective-permute-start
  5244.5 43.5 all-reduce.1
  5288.7 16.7 concatenate.17
  5305.4 20.1 multiply_reduce_fusion.4
  5333.5 4.6 stack.132
  5338.1 38.7 all-reduce.4
  5380.5 11.7 multiply_reduce_fusion.3
  5406.3 41.8 all-reduce.3
  5458.4 9.9 multiply_subtract_fusion
  (381 shorter events, 123.0 us)
Async XLA Ops:
  7.2 794.7 %all-gather.19.cloned.1.call-start = ((), (), s32[]{:S(2)}) async-start(), calls=%async_computation.17 | async-start | bytes 79884288 | tf_op jit(solution)/shard_map/all_gather | solution.py:232
  11.4 897.7 %all-gather.9.cloned.1.call-start = ((), (), s32[]{:S(2)}) async-start(), calls=%async_computation.7 | async-start | bytes 3649536 | tf_op jit(solution)/shard_map/all_gather | solution.py:234
  12.2 963.5 %all-gather.11.cloned.1.call-start = ((), (), s32[]{:S(2)}) async-start(), calls=%async_computation.8 | async-start | bytes 1216512 | tf_op jit(solution)/shard_map/all_gather | solution.py:235
  12.9 969.0 %all-gather.13.cloned.1.call-start = ((), (), s32[]{:S(2)}) async-start(), calls=%async_computation.9 | async-start | bytes 4866048 | tf_op jit(solution)/shard_map/all_gather | solution.py:236
  102.3 624.0 %copy-start.113 = (s32[2]{0:T(128)S(1)}, s32[2]{0:T(128)}, u32[]{:S(2)}) copy-start(s32[2]{0:T(128)} %param.29) | copy-start | bytes 28
  102.3 625.7 %copy-start.46 = (f32[512,24]{0,1:T(8,128)S(1)}, f32[512,24]{0,1:T(8,128)}, u32[]{:S(2)}) copy-start(f32[512,24]{0,1:T(8,128)} %param.34) | copy-start | bytes 147460
  102.4 937.2 %all-to-all-start = ((bf16[32,2,100608]{2,1,0:T(2,128)(2,1)}), bf16[32,2,100608]{2,1,0:T(2,128)(2,1)}, u32[]{:S(2)}, u32[]{:S(2)}) async-start(bf16[32,2,100608]{2,1,0:T(2,128)(2,1)} %reshape.489), calls=%async_computation | async-start | bytes 25755648 | tf_op jit(solution)/shard_map/all_to_all | solution.py:264
  109.7 910.5 %all-gather.15.cloned.1.call-start = ((), (), s32[]{:S(2)}) async-start(), calls=%async_computation.10 | async-start | bytes 4866048 | tf_op jit(solution)/shard_map/all_gather | solution.py:237
  110.4 1057.0 %all-gather.17.cloned.1.call-start = ((), (), s32[]{:S(2)}) async-start(), calls=%async_computation.11 | async-start | bytes 6488064 | tf_op jit(solution)/shard_map/all_gather | solution.py:263
  111.1 794.3 %copy-start.67 = (pred[2,512]{1,0:T(4,128)(4,1)}, pred[2,512]{1,0:T(4,128)(4,1)S(1)}, u32[]{:S(2)}) copy-start(pred[2,512]{1,0:T(4,128)(4,1)S(1)} %compare_and_fusion) | copy-start | bytes 3076
  111.1 849.8 %copy-start.70 = (pred[2,512]{1,0:T(4,128)(4,1)}, pred[2,512]{1,0:T(4,128)(4,1)S(1)}, u32[]{:S(2)}) copy-start(pred[2,512]{1,0:T(4,128)(4,1)S(1)} %broadcast_compare_fusion) | copy-start | bytes 3076
  726.3 293.8 %copy-start.79 = (f32[768]{0:T(1024)}, f32[768]{0:T(1024)S(1)}, u32[]{:S(2)}) copy-start(f32[768]{0:T(1024)S(1)} %get-tuple-element.99) | copy-start | bytes 9220
  726.3 304.8 %copy-start.59 = (f32[768]{0:T(1024)}, f32[768]{0:T(1024)S(1)}, u32[]{:S(2)}) copy-start(f32[768]{0:T(1024)S(1)} %get-tuple-element.105) | copy-start | bytes 9220
  801.8 229.3 %copy-start.2 = (f32[512,768]{1,0:T(8,128)}, f32[512,768]{1,0:T(8,128)S(1)}, u32[]{:S(2)}) copy-start(f32[512,768]{1,0:T(8,128)S(1)} %copy.130) | copy-start | bytes 4718596
  904.7 126.4 %copy-start = (bf16[1024,768]{1,0:T(8,128)(2,1)}, bf16[1024,768]{1,0:T(8,128)(2,1)S(1)}, u32[]{:S(2)}) copy-start(bf16[1024,768]{1,0:T(8,128)(2,1)S(1)} %gather_fusion) | copy-start | bytes 4718596
  938.1 22.9 copy-start.21
  981.9 38.2 copy-start.86
  981.9 38.2 copy-start.106
  1039.5 329.1 %reduce-scatter.12.cloned.1.call-start = ((), (), s32[]{:S(2)}) async-start(), calls=%async_computation.12 | async-start | bytes 12976128 | tf_op jit(solution)/shard_map/reduce_scatter | solution.py:271
  1215.7 152.9 %copy-start.8 = (f32[2,512,768]{2,1,0:T(8,128)S(1)}, f32[2,512,768]{2,1,0:T(8,128)}, u32[]{:S(2)}) copy-start(f32[2,512,768]{2,1,0:T(8,128)} %get-tuple-element.140) | copy-start | bytes 9437188
  1215.7 4109.8 %reduce-scatter.22.cloned.1.call-start = ((), (), s32[]{:S(2)}) async-start(), calls=%async_computation.18 | async-start | bytes 1622016
  1389.3 18.9 copy-start.5
  1465.4 21.7 copy-start.16
  1539.0 3788.1 %reduce-scatter.16.cloned.1.call-start = ((), (), s32[]{:S(2)}) async-start(), calls=%async_computation.14 | async-start | bytes 2433024 | tf_op jit(solution)/shard_map/reduce_scatter | solution.py:297
  1544.0 3784.7 %reduce-scatter.14.cloned.1.call-start = ((), (), s32[]{:S(2)}) async-start(), calls=%async_computation.13 | async-start | bytes 7299072 | tf_op jit(solution)/shard_map/reduce_scatter | solution.py:296
  1553.8 3776.4 %reduce-scatter.18.cloned.1.call-start = ((), (), s32[]{:S(2)}) async-start(), calls=%async_computation.15 | async-start | bytes 9732096 | tf_op jit(solution)/shard_map/reduce_scatter | solution.py:298
  1565.2 3766.7 %reduce-scatter.20.cloned.1.call-start = ((), (), s32[]{:S(2)}) async-start(), calls=%async_computation.16 | async-start | bytes 9732096 | tf_op jit(solution)/shard_map/reduce_scatter | solution.py:299
  1565.8 48.7 copy-start.11
  1745.8 103.4 %copy-start.29 = (bf16[1024,768]{1,0:T(8,128)(2,1)S(1)}, bf16[1024,768]{1,0:T(8,128)(2,1)}, u32[]{:S(2)}) copy-start(bf16[1024,768]{1,0:T(8,128)(2,1)} %get-tuple-element.130) | copy-start | bytes 4718596
  1859.4 3380.3 %copy-start.91 = (s32[2,512]{1,0:T(2,128)S(1)}, s32[2,512]{1,0:T(2,128)}, u32[]{:S(2)}) copy-start(s32[2,512]{1,0:T(2,128)} %param.28) | copy-start | bytes 12292
  1859.4 3380.3 %copy-start.14 = (f32[2,512,768]{2,1,0:T(8,128)S(1)}, f32[2,512,768]{2,1,0:T(8,128)}, u32[]{:S(2)}) copy-start(f32[2,512,768]{2,1,0:T(8,128)} %get-tuple-element.141) | copy-start | bytes 9437188
  5234.3 54.5 collective-permute-start
  5305.4 74.1 %copy-start.73 = (f32[14,24]{1,0:T(8,128)S(1)}, f32[14,24]{1,0:T(8,128)}, u32[]{:S(2)}) copy-start(f32[14,24]{1,0:T(8,128)} %param.39) | copy-start | bytes 4036
  5305.4 74.2 %copy-start.103 = (f32[14,24]{1,0:T(8,128)S(1)}, f32[14,24]{1,0:T(8,128)}, u32[]{:S(2)}) copy-start(f32[14,24]{1,0:T(8,128)} %param.46) | copy-start | bytes 4036
  5305.4 74.2 %copy-start.104 = (f32[14,24]{1,0:T(8,128)S(1)}, f32[14,24]{1,0:T(8,128)}, u32[]{:S(2)}) copy-start(f32[14,24]{1,0:T(8,128)} %param.53) | copy-start | bytes 4036
  5380.3 73.5 %copy-start.92 = (f32[14,24]{1,0:T(8,128)}, f32[14,24]{1,0:T(8,128)S(1)}, u32[]{:S(2)}) copy-start(f32[14,24]{1,0:T(8,128)S(1)} %get-tuple-element.113) | copy-start | bytes 4036
  5380.3 73.5 %copy-start.93 = (f32[14,24]{1,0:T(8,128)}, f32[14,24]{1,0:T(8,128)S(1)}, u32[]{:S(2)}) copy-start(f32[14,24]{1,0:T(8,128)S(1)} %get-tuple-element.114) | copy-start | bytes 4036
  5380.5 14.0 copy-start.24
  5392.9 63.7 %copy-start.62 = (f32[512,24]{0,1:T(8,128)}, f32[512,24]{0,1:T(8,128)S(1)}, u32[]{:S(2)}) copy-start(f32[512,24]{0,1:T(8,128)S(1)} %get-tuple-element.123) | copy-start | bytes 147460
  5392.9 63.7 %copy-start.63 = (f32[512,24]{0,1:T(8,128)}, f32[512,24]{0,1:T(8,128)S(1)}, u32[]{:S(2)}) copy-start(f32[512,24]{0,1:T(8,128)S(1)} %get-tuple-element.124) | copy-start | bytes 147460
  5393.6 63.0 %copy-start.53 = (f32[24,768]{1,0:T(8,128)}, f32[24,768]{1,0:T(8,128)S(1)}, u32[]{:S(2)}) copy-start(f32[24,768]{1,0:T(8,128)S(1)} %get-tuple-element.119) | copy-start | bytes 221188
  5393.6 63.0 %copy-start.54 = (f32[24,768]{1,0:T(8,128)}, f32[24,768]{1,0:T(8,128)S(1)}, u32[]{:S(2)}) copy-start(f32[24,768]{1,0:T(8,128)S(1)} %get-tuple-element.120) | copy-start | bytes 221188
  5394.5 63.9 %copy-start.40 = (f32[24,2304]{1,0:T(8,128)}, f32[24,2304]{1,0:T(8,128)S(1)}, u32[]{:S(2)}) copy-start(f32[24,2304]{1,0:T(8,128)S(1)} %get-tuple-element.121) | copy-start | bytes 663556
  5394.5 63.9 %copy-start.41 = (f32[24,2304]{1,0:T(8,128)}, f32[24,2304]{1,0:T(8,128)S(1)}, u32[]{:S(2)}) copy-start(f32[24,2304]{1,0:T(8,128)S(1)} %get-tuple-element.122) | copy-start | bytes 663556
  5395.5 72.9 %copy-start.34 = (f32[96,768]{1,0:T(8,128)}, f32[96,768]{1,0:T(8,128)S(1)}, u32[]{:S(2)}) copy-start(f32[96,768]{1,0:T(8,128)S(1)} %get-tuple-element.115) | copy-start | bytes 884740
  5395.5 72.9 %copy-start.35 = (f32[96,768]{1,0:T(8,128)}, f32[96,768]{1,0:T(8,128)S(1)}, u32[]{:S(2)}) copy-start(f32[96,768]{1,0:T(8,128)S(1)} %get-tuple-element.116) | copy-start | bytes 884740
  5396.4 71.9 %copy-start.36 = (f32[24,3072]{1,0:T(8,128)}, f32[24,3072]{1,0:T(8,128)S(1)}, u32[]{:S(2)}) copy-start(f32[24,3072]{1,0:T(8,128)S(1)} %get-tuple-element.117) | copy-start | bytes 884740
  5396.4 71.9 %copy-start.37 = (f32[24,3072]{1,0:T(8,128)}, f32[24,3072]{1,0:T(8,128)S(1)}, u32[]{:S(2)}) copy-start(f32[24,3072]{1,0:T(8,128)S(1)} %get-tuple-element.118) | copy-start | bytes 884740
  (80 other events, 561.4 us)
Sparse Core Ops, SparseCore 0:
  11.5 672.7 all-gather.18
  687.7 60.0 all-gather.8
  751.1 53.4 all-gather.10
  807.9 62.4 all-gather.12
  873.5 62.3 all-gather.14
  1039.6 67.1 all-gather.16
  1215.8 152.6 reduce-scatter.11
  1539.2 96.0 reduce-scatter.21
  1641.4 97.9 reduce-scatter.15
  1745.0 118.1 reduce-scatter.13
  1870.1 173.9 reduce-scatter.17
  2049.8 174.3 reduce-scatter.19
where the time goes:
time: 5500 us; the launch traced here: 5480 us
  blocking collectives  4180 us (76%)
  local copies, waits for them, and re-layouts  569 us (10%)
  matrix products  270 us (5%)
  other arithmetic  264 us (5%)
  waiting for transfers between devices  152 us (3%)
    unnamed x2, blocking collectives  3420 us
    all_gather x1, blocking collectives, on_device(): lax.all_gather(lowered[6], ('dp', 'fsdp'), axis=1, tiled=True)  613 us
    unnamed x242, local copies, waits for them, and re-layouts  255 us
    reduce_scatter x1, waiting for transfers between devices, on_device(): lax.psum_scatter(dense(grad_logits, lowered[0]), ('dp', 'fsdp'), scatter_...  152 us
    scatter-add x1, other arithmetic, on_device(): jax.ops.segment_sum(flat_grad, slot_ids, num_segments=count_rows + 1)  131 us
  transfers between devices with their start and end apart: 14, of which 1 were waited for; matrix products, arithmetic and copies ran while one was open for 77% of the time, Pallas kernels for 0%

commit v1 on v0

v1 whole, which is shorter than its diff:
```python
import functools

import jax
import jax.numpy as jnp
from jax import lax
from jax.experimental import pallas as pl
from jax.experimental.pallas import tpu as pltpu
from jax.sharding import Mesh
from jax.sharding import PartitionSpec as P

H = 12
HD = 64
STEP = 10


NORM_EPS = 1e-05
CLIP_NORM = 0.5
BETA_ONE = 0.9
BETA_TWO = 0.999
ADAM_EPS = 1e-06
DECAY_RATE = 0.01
LEARN_RATE = 0.3
MASKED_SCORE = -1e30

SPLIT = ("plane", "pair")
AXES = ("plane", "pair", "fsdp")
VMEM = 60 * 2**20


def norm_rows(values, gain_row, shift_row):
    row_mean = jnp.mean(values, axis=-1, keepdims=True)
    centered = values - row_mean
    row_var = jnp.mean(centered * centered, axis=-1, keepdims=True)
    return centered * lax.rsqrt(row_var + NORM_EPS) * gain_row + shift_row


def normal_cdf(values):
    return 0.5 + 0.5 * lax.erf(values * 0.5**0.5)


def gelu_slope(values):
    density = jnp.exp(-0.5 * values * values) * (2.0 * jnp.pi) ** -0.5
    return normal_cdf(values) + values * density


def dense(left_op, right_op):
    return jnp.dot(left_op, right_op, preferred_element_type=jnp.float32)


def dense_tn(left_op, right_op):
    return lax.dot_general(
        left_op, right_op, (((0,), (0,)), ((), ())), preferred_element_type=jnp.float32
    )


def dense_nt(left_op, right_op):
    return lax.dot_general(
        left_op, right_op, (((1,), (1,)), ((), ())), preferred_element_type=jnp.float32
    )


def pair_lanes(shape, member):
    lane = lax.broadcasted_iota(jnp.int32, shape, 1)
    return (lane >= HD) if member else (lane < HD)


def softmax_rows(query_rows, key_rows, length):
    scores = dense_nt(query_rows, key_rows)
    spot = lax.broadcasted_iota(jnp.int32, scores.shape, 1)
    scores = jnp.where(spot < length, scores, MASKED_SCORE)
    exponent = jnp.exp(scores - jnp.max(scores, axis=1, keepdims=True))
    return exponent / jnp.sum(exponent, axis=1, keepdims=True)


def row_spans(seq_len):
    half = seq_len // 2
    return ((0, half), (half, seq_len))


def mix_kernel(length_ref, query_ref, key_ref, value_ref, mixed_ref):
    seq_len = query_ref.shape[0]
    length = length_ref[pl.program_id(0)]

    for low, high in row_spans(seq_len):

        @pl.when((length > low) & (length <= high))
        def _():
            step = high // 2 if low else high
            keys, values = key_ref[0:high, :], value_ref[0:high, :]
            for row in range(0, high, step):
                queries = query_ref[row : row + step, :] * 0.125
                parts = []
                for member in (0, 1):
                    lanes = pair_lanes(queries.shape, member)
                    chance = softmax_rows(
                        jnp.where(lanes, queries, jnp.zeros_like(queries)), keys, length
                    )
                    parts.append(dense(chance.astype(jnp.bfloat16), values))
                mixed_ref[row : row + step, :] = jnp.where(
                    pair_lanes(parts[0].shape, 1), parts[1], parts[0]
                ).astype(jnp.bfloat16)
            if high < seq_len:
                mixed_ref[high:, :] = jnp.zeros((seq_len - high, 2 * HD), jnp.bfloat16)

    @pl.when(length == 0)
    def _():
        mixed_ref[...] = jnp.zeros_like(mixed_ref)


def unmix_kernel(
    length_ref, query_ref, key_ref, value_ref, grad_ref, query_out, key_out, value_out
):
    seq_len = query_ref.shape[0]
    length = length_ref[pl.program_id(0)]
    outs = (query_out, key_out, value_out)

    for low, high in row_spans(seq_len):

        @pl.when((length > low) & (length <= high))
        def _():
            step = high // 2 if low else high
            keys, values = key_ref[0:high, :], value_ref[0:high, :]
            key_total, value_total = None, None
            for row in range(0, high, step):
                plain = query_ref[row : row + step, :]
                queries = plain * 0.125
                grads = grad_ref[row : row + step, :]
                parts = []
                for member in (0, 1):
                    lanes = pair_lanes(queries.shape, member)
                    zero = jnp.zeros_like(queries)
                    chance = softmax_rows(jnp.where(lanes, queries, zero), keys, length)
                    slope = dense_nt(jnp.where(lanes, grads, zero), values)
                    slope = chance * (slope - jnp.sum(slope * chance, axis=1, keepdims=True))
                    slope = slope.astype(jnp.bfloat16)
                    parts.append(
                        (
                            dense(slope, keys),
                            dense_tn(slope, plain),
                            dense_tn(chance.astype(jnp.bfloat16), grads),
                        )
                    )
                query_part, key_part, value_part = [
                    jnp.where(pair_lanes(first.shape, 1), second, first)
                    for first, second in zip(*parts)
                ]
                query_out[row : row + step, :] = (query_part * 0.125).astype(jnp.bfloat16)
                key_total = key_part if key_total is None else key_total + key_part
                value_total = value_part if value_total is None else value_total + value_part
            key_out[0:high, :] = (key_total * 0.125).astype(jnp.bfloat16)
            value_out[0:high, :] = value_total.astype(jnp.bfloat16)
            if high < seq_len:
                for ref in outs:
                    ref[high:, :] = jnp.zeros((seq_len - high, 2 * HD), jnp.bfloat16)

    @pl.when(length == 0)
    def _():
        for ref in outs:
            ref[...] = jnp.zeros_like(ref)


def attend(lengths, packed, grad_mixed=None):
    seq_count = lengths.shape[0]
    seq_len = packed.shape[0] // seq_count
    pairs = H // 2

    def block(first):
        return pl.BlockSpec((seq_len, 2 * HD), lambda s, h, _: (s, first + h))

    out = jax.ShapeDtypeStruct((packed.shape[0], H * HD), jnp.bfloat16)
    forward = grad_mixed is None
    operands = (packed, packed, packed) + (() if forward else (grad_mixed,))
    products = seq_count * H * seq_len * seq_len
    return pl.pallas_call(
        mix_kernel if forward else unmix_kernel,
        out_shape=out if forward else (out, out, out),
        grid_spec=pltpu.PrefetchScalarGridSpec(
            num_scalar_prefetch=1,
            grid=(seq_count, pairs),
            in_specs=[block(0), block(pairs), block(2 * pairs)] + ([] if forward else [block(0)]),
            out_specs=block(0) if forward else (block(0),) * 3,
        ),
        compiler_params=pltpu.CompilerParams(vmem_limit_bytes=VMEM),
        cost_estimate=pl.CostEstimate(
            flops=products * HD * (16 if forward else 40),
            bytes_accessed=packed.shape[0] * H * HD * (8 if forward else 14),
            transcendentals=products,
        ),
    )(lengths, *operands)


def parcel_kernel(own_rows, tiles, wide, source, parcel_ref, slots, sems):
    part, parts = pl.program_id(0), pl.num_programs(0)

    def first_tile(index):
        return jnp.minimum(own_rows * index // 128, tiles - wide)

    def fetch(index):
        lane = pl.multiple_of(first_tile(index) * 128, 128)
        slot = lax.rem(index, 2)
        return pltpu.make_async_copy(
            source.at[:, pl.ds(lane, wide * 128)], slots.at[slot], sems.at[slot]
        )

    @pl.when(part == 0)
    def _():
        fetch(0).start()

    @pl.when(part + 1 < parts)
    def _():
        fetch(part + 1).start()

    fetch(part).wait()
    shift = own_rows * part - 128 * first_tile(part)
    width = parcel_ref.shape[2]
    values = slots[lax.rem(part, 2)].astype(jnp.float32)
    values = pltpu.roll(values, lax.rem(wide * 128 - shift, wide * 128), axis=1)[:, :width]
    lane = lax.broadcasted_iota(jnp.int32, values.shape, 1)
    parcel_ref[0] = jnp.where(lane < own_rows, values, 0.0).astype(jnp.bfloat16)


def parcels_of(flat_teacher, own_rows, padded, n_dev):
    n_pick, vocab = flat_teacher.shape
    tiles = vocab // 128
    wide = min(tiles, max((own_rows * r % 128 + padded + 127) // 128 for r in range(n_dev)))
    return pl.pallas_call(
        functools.partial(parcel_kernel, own_rows, tiles, wide),
        out_shape=jax.ShapeDtypeStruct((n_dev, n_pick, padded), jnp.bfloat16),
        grid=(n_dev,),
        in_specs=[pl.BlockSpec(memory_space=pl.ANY)],
        out_specs=pl.BlockSpec((1, n_pick, padded), lambda r: (r, 0, 0)),
        scratch_shapes=[
            pltpu.VMEM((2, n_pick, wide * 128), jnp.bfloat16),
            pltpu.SemaphoreType.DMA((2,)),
        ],
        compiler_params=pltpu.CompilerParams(vmem_limit_bytes=VMEM),
        cost_estimate=pl.CostEstimate(
            flops=4 * n_pick * vocab, bytes_accessed=4 * n_pick * vocab, transcendentals=0
        ),
    )(flat_teacher)


def head_kernel(n_fs, place_ref, chosen_ref, target_ref, *refs):
    tables = refs[:n_fs]
    slope_ref, part_ref, loss_ref = refs[n_fs:]
    chosen = chosen_ref[...]
    senders, _, n_pick, width = target_ref.shape
    total, loss = None, None
    for step in range(n_fs):
        table = tables[step][...]
        target = target_ref[:, place_ref[step]].reshape(senders * n_pick, width)
        gap = dense_nt(chosen, table) - target.astype(jnp.float32)
        square = jnp.sum((gap * gap).reshape(-1, 8, width), axis=0)
        loss = square if loss is None else loss + square
        slope = (2.0 * gap).astype(jnp.bfloat16)
        slope_ref[step] = slope
        part = dense(slope, table)
        total = part if total is None else total + part
    part_ref[...] = total.astype(part_ref.dtype)

    @pl.when(pl.program_id(0) == 0)
    def _():
        loss_ref[...] = jnp.zeros_like(loss_ref)

    loss_ref[...] += loss


def head_products(places, all_chosen, targets, tables):
    n_dp, n_fs, n_pick, padded = targets.shape
    row_width = all_chosen.shape[1]
    rows = 2 * n_pick
    whole = pl.BlockSpec((padded, row_width), lambda m, _: (0, 0))
    return pl.pallas_call(
        functools.partial(head_kernel, n_fs),
        out_shape=(
            jax.ShapeDtypeStruct((n_fs, n_dp * n_pick, padded), jnp.bfloat16),
            jax.ShapeDtypeStruct((n_dp * n_pick, row_width), jnp.bfloat16),
            jax.ShapeDtypeStruct((8, padded), jnp.float32),
        ),
        grid_spec=pltpu.PrefetchScalarGridSpec(
            num_scalar_prefetch=1,
            grid=(n_dp // 2,),
            in_specs=[
                pl.BlockSpec((rows, row_width), lambda m, _: (m, 0)),
                pl.BlockSpec((2, n_fs, n_pick, padded), lambda m, _: (m, 0, 0, 0)),
            ]
            + [whole] * n_fs,
            out_specs=(
                pl.BlockSpec((n_fs, rows, padded), lambda m, _: (0, m, 0)),
                pl.BlockSpec((rows, row_width), lambda m, _: (m, 0)),
                pl.BlockSpec((8, padded), lambda m, _: (0, 0)),
            ),
        ),
        compiler_params=pltpu.CompilerParams(vmem_limit_bytes=VMEM),
        cost_estimate=pl.CostEstimate(
            flops=4 * n_dp * n_pick * n_fs * padded * row_width,
            bytes_accessed=4 * n_dp * n_pick * n_fs * padded + 2 * n_fs * padded * row_width,
            transcendentals=0,
        ),
    )(places, all_chosen, targets, *tables)


def sum_to_owners(values):
    n_plane, n_fs = lax.axis_size("plane"), lax.axis_size("fsdp")
    member = lax.axis_index("pair")
    rows, width = values.shape
    shaped = values.reshape(n_plane, 2, rows // (2 * n_plane), width)
    kept = lax.dynamic_index_in_dim(shaped, member, 1, False)
    given = lax.dynamic_index_in_dim(shaped, 1 - member, 1, False)
    got = lax.ppermute(given, "pair", [(0, 1), (1, 0)])
    part = (kept.astype(jnp.float32) + got.astype(jnp.float32)).astype(jnp.bfloat16)
    part = lax.all_to_all(part, "plane", split_axis=0, concat_axis=0)
    part = jnp.sum(part.astype(jnp.float32), axis=0).astype(jnp.bfloat16)
    part = part.reshape(n_fs, -1, width)
    part = lax.all_to_all(part, "fsdp", split_axis=0, concat_axis=0)
    return jnp.sum(part.astype(jnp.float32), axis=0)


def total_over(values, axes):
    n_dev = lax.axis_size(axes)
    tile = jnp.zeros((8, 128), jnp.float32).at[0, : values.shape[0]].set(values)
    every = lax.all_to_all(
        jnp.broadcast_to(tile[None], (n_dev, 8, 128)), axes, split_axis=0, concat_axis=0
    )
    return jnp.sum(every, axis=0)[0, : values.shape[0]]


def route_plan(ids, live, own_rows, n_dev):
    place = jnp.arange(ids.shape[0])
    owner = ids // own_rows
    same = (ids[:, None] == ids[None, :]) & live[None, :]
    leader = jnp.min(jnp.where(same, place[None, :], ids.shape[0]), axis=1)
    first = live & (leader == place)
    before = (owner[:, None] == owner[None, :]) & (place[None, :] < leader[:, None])
    rank = jnp.sum(before & first[None, :], axis=1, dtype=jnp.int32)
    room = max(16, 1280 // n_dev)
    rounds = jnp.max(jnp.where(first, rank, 0)) // room + 1
    return ids, live, owner, first, rank, room, rounds, own_rows, n_dev


def slots_of(plan, turn):
    ids, live, owner, first, rank, room, rounds, own_rows, n_dev = plan
    here = live & (rank >= turn * room) & (rank < (turn + 1) * room)
    return jnp.where(here, owner * room + rank - turn * room, -1)


def exchange_wanted(plan, turn, axes):
    ids, live, owner, first, rank, room, rounds, own_rows, n_dev = plan
    slots = slots_of(plan, turn)
    local = jnp.where(first, ids - owner * own_rows + 1, 0)
    hit = jnp.arange(n_dev * room)[:, None] == slots[None, :]
    asked = jnp.max(jnp.where(hit, local[None, :], 0), axis=1) - 1
    message = jnp.concatenate(
        [
            asked.reshape(n_dev, room),
            jnp.broadcast_to(rounds, (n_dev, 128 - room)).astype(jnp.int32),
        ],
        axis=1,
    ).reshape(n_dev, 1, 128)
    heard = lax.all_to_all(message, axes, split_axis=0, concat_axis=0).reshape(n_dev, 128)
    return heard[:, :room].reshape(-1), jnp.max(heard[:, room:])


def fetch_rows(plan, turn, wanted, table_low, axes):
    room, own_rows, n_dev = plan[5], plan[7], plan[8]
    one_hot = (wanted[:, None] == jnp.arange(own_rows)[None, :]).astype(jnp.bfloat16)
    rows = dense(one_hot, table_low).astype(jnp.bfloat16)
    rows = lax.all_to_all(rows.reshape(n_dev, room, -1), axes, split_axis=0, concat_axis=0)
    back = (slots_of(plan, turn)[:, None] == jnp.arange(n_dev * room)[None, :]).astype(
        jnp.bfloat16
    )
    return dense(back, rows.reshape(n_dev * room, -1))


def more_rows(plan, rounds, token_rows, table_low, axes):
    def body(state):
        turn, total = state
        wanted, _ = exchange_wanted(plan, turn, axes)
        return turn + 1, total + fetch_rows(plan, turn, wanted, table_low, axes)

    return lax.while_loop(lambda state: state[0] < rounds, body, (jnp.int32(1), token_rows))[1]


def send_rows(plan, turn, wanted, flat_grad, own_rows, axes):
    room, n_dev = plan[5], plan[8]
    spread = (jnp.arange(n_dev * room)[:, None] == slots_of(plan, turn)[None, :]).astype(
        jnp.bfloat16
    )
    high = flat_grad.astype(jnp.bfloat16)
    rest = (flat_grad - high.astype(jnp.float32)).astype(jnp.bfloat16)
    sums = (dense(spread, high) + dense(spread, rest)).astype(jnp.bfloat16)
    got = lax.all_to_all(sums.reshape(n_dev, room, -1), axes, split_axis=0, concat_axis=0)
    one_hot = (jnp.arange(own_rows)[:, None] == wanted[None, :]).astype(jnp.bfloat16)
    return dense(one_hot, got.reshape(n_dev * room, -1))


def more_sent(plan, rounds, term_rows, flat_grad, own_rows, axes):
    def body(state):
        turn, total = state
        wanted, _ = exchange_wanted(plan, turn, axes)
        return turn + 1, total + send_rows(plan, turn, wanted, flat_grad, own_rows, axes)

    return lax.while_loop(lambda state: state[0] < rounds, body, (jnp.int32(1), term_rows))[1]


def layer_forward(layer_inputs, lengths, matrices, vector_params):
    qkv_low, out_low, up_low, down_low = matrices
    row_width = layer_inputs.shape[2]
    flat_in = layer_inputs.reshape(-1, row_width)
    flat_low = flat_in.astype(jnp.bfloat16)
    qkv_bias = jnp.concatenate(
        [vector_params[2], jnp.zeros_like(vector_params[2]), vector_params[3]]
    )
    packed = (dense(flat_low, qkv_low) + qkv_bias).astype(jnp.bfloat16)
    mixed_output = attend(lengths, packed)
    joined_one = flat_in + (dense(mixed_output, out_low) + vector_params[4])
    first_normed = norm_rows(joined_one, vector_params[5], vector_params[6])
    normed_low = first_normed.astype(jnp.bfloat16)
    hidden_state = dense(normed_low, up_low) + vector_params[10:14].reshape(-1)
    gelu_activated = (hidden_state * normal_cdf(hidden_state)).astype(jnp.bfloat16)
    joined_two = first_normed + (dense(gelu_activated, down_low) + vector_params[7])
    result = norm_rows(joined_two, vector_params[8], vector_params[9]).reshape(layer_inputs.shape)
    saved_state = (
        flat_low,
        packed,
        mixed_output,
        joined_one,
        normed_low,
        hidden_state,
        gelu_activated,
        joined_two,
    )
    return (result, saved_state)


def layer_backward(grad_out, lengths, matrices, vector_params, saved_state):
    qkv_low, out_low, up_low, down_low = matrices
    (
        flat_low,
        packed,
        mixed_output,
        joined_one,
        normed_low,
        hidden_state,
        gelu_activated,
        joined_two,
    ) = saved_state
    row_width = flat_low.shape[1]
    _, back_two = jax.vjp(norm_rows, joined_two, vector_params[8], vector_params[9])
    grad_joined_two, gain_two, shift_two = back_two(grad_out)
    grad_feed = grad_joined_two.astype(jnp.bfloat16)
    grad_hidden = (dense_nt(grad_feed, down_low) * gelu_slope(hidden_state)).astype(jnp.bfloat16)
    down_grad = dense_tn(gelu_activated, grad_feed).astype(jnp.bfloat16)
    up_grad = dense_tn(normed_low, grad_hidden).astype(jnp.bfloat16)
    grad_normed = grad_joined_two + dense_nt(grad_hidden, up_low)
    _, back_one = jax.vjp(norm_rows, joined_one, vector_params[5], vector_params[6])
    grad_joined_one, gain_one, shift_one = back_one(grad_normed)
    grad_attention = grad_joined_one.astype(jnp.bfloat16)
    grad_mixed = dense_nt(grad_attention, out_low).astype(jnp.bfloat16)
    out_grad = dense_tn(mixed_output, grad_attention).astype(jnp.bfloat16)
    grad_mixed, down_grad, up_grad, out_grad = lax.optimization_barrier(
        (grad_mixed, down_grad, up_grad, out_grad)
    )
    down_sum, up_sum, out_sum = [sum_to_owners(g) for g in (down_grad, up_grad, out_grad)]
    grad_packed = jnp.concatenate(attend(lengths, packed, grad_mixed), axis=1)
    grad_inputs = grad_joined_one + dense_nt(grad_packed, qkv_low)
    matrix_grads = (
        dense_tn(flat_low, grad_packed).astype(jnp.bfloat16),
        out_sum,
        up_sum,
        down_sum,
    )
    packed_sum = jnp.sum(grad_packed, axis=0, dtype=jnp.float32)
    vector_rows = jnp.stack(
        [
            packed_sum[:row_width],
            packed_sum[2 * row_width :],
            jnp.sum(grad_attention, axis=0, dtype=jnp.float32),
            gain_one,
            shift_one,
            jnp.sum(grad_feed, axis=0, dtype=jnp.float32),
            gain_two,
            shift_two,
        ]
    )
    up_rows = jnp.sum(grad_hidden, axis=0, dtype=jnp.float32).reshape(4, row_width)
    return (grad_inputs, matrix_grads, jnp.concatenate([vector_rows, up_rows]))


def on_device(
    token_ids,
    true_mask,
    keep_layer,
    picked,
    teacher_hidden,
    teacher_logits,
    embed_table,
    pos_table,
    query_key_value_weight,
    output_weight,
    up_weight,
    down_weight,
    gains_biases,
    first_embed,
    first_pos,
    first_qkv,
    first_out,
    first_up,
    first_down,
    first_gains,
    second_embed,
    second_pos,
    second_qkv,
    second_out,
    second_up,
    second_down,
    second_gains,
):
    axes = AXES
    n_dp, n_fs = lax.axis_size(SPLIT), lax.axis_size("fsdp")
    n_dev = n_dp * n_fs
    i_fs = lax.axis_index("fsdp")
    masters = (
        embed_table,
        pos_table,
        query_key_value_weight,
        output_weight,
        up_weight,
        down_weight,
        gains_biases,
    )
    firsts = (first_embed, first_pos, first_qkv, first_out, first_up, first_down, first_gains)
    seconds = (
        second_embed,
        second_pos,
        second_qkv,
        second_out,
        second_up,
        second_down,
        second_gains,
    )
    seq_count, seq_len = token_ids.shape
    own_rows, row_width = embed_table.shape
    ff = up_weight.shape[1]
    in_rows = query_key_value_weight.shape[0]
    n_tok = seq_count * seq_len
    n_pick = picked.shape[0] * picked.shape[1]
    vocab = own_rows * n_dev
    block_rows = own_rows * n_fs

    table_low = embed_table.astype(jnp.bfloat16)
    pack_width = 3 * row_width + row_width + ff + ff + seq_len
    gain_width = -(-14 // 128) * 128
    packed_low = jnp.concatenate(
        [
            query_key_value_weight,
            output_weight,
            up_weight,
            down_weight.reshape(in_rows, ff),
            pos_table.T,
            jnp.pad(gains_biases.T, ((0, 0), (0, gain_width - 14))),
        ],
        axis=1,
    ).astype(jnp.bfloat16)
    gathered = lax.all_gather(packed_low, axes, axis=0, tiled=True)
    qkv_full = gathered[:, : 3 * row_width]
    out_full = gathered[:, 3 * row_width : 4 * row_width]
    up_full = gathered[:, 4 * row_width : 4 * row_width + ff]
    down_full = gathered[:, 4 * row_width + ff : 4 * row_width + 2 * ff].reshape(ff, row_width)
    pos_full = gathered[:, 4 * row_width + 2 * ff : pack_width].astype(jnp.float32).T
    vector_params = gathered[:, pack_width : pack_width + 14].astype(jnp.float32).T
    matrices = (qkv_full, out_full, up_full, down_full)

    plan = route_plan(token_ids.reshape(-1), true_mask.reshape(-1) > 0, own_rows, n_dev)
    wanted, rounds = exchange_wanted(plan, 0, axes)
    token_rows = fetch_rows(plan, 0, wanted, table_low, axes)
    token_rows = more_rows(plan, rounds, token_rows, table_low, axes)

    padded = -(-own_rows // 16) * 16
    targets = parcels_of(teacher_logits.reshape(n_pick, vocab), own_rows, padded, n_dev)
    targets = lax.all_to_all(
        targets.reshape(n_dp, n_fs, n_pick, padded), SPLIT, split_axis=0, concat_axis=0
    )
    ring = [(z, (z + 1) % n_fs) for z in range(n_fs)]
    tables = [jnp.pad(table_low, ((0, padded - own_rows), (0, 0)))]
    for _ in range(n_fs - 1):
        tables.append(lax.ppermute(tables[-1], "fsdp", ring))
    places = lax.rem(i_fs - jnp.arange(n_fs, dtype=jnp.int32) + n_fs, n_fs)

    embedded = token_rows.reshape(seq_count, seq_len, row_width) + pos_full[None]
    layer_inputs = norm_rows(embedded, vector_params[0], vector_params[1])
    lengths = jnp.sum(true_mask, axis=1) * (keep_layer > 0)
    layer_out, saved_state = layer_forward(layer_inputs, lengths, matrices, vector_params)
    keep_rows = (keep_layer > 0)[:, None, None]
    final_rows = jnp.where(keep_rows, layer_out, layer_inputs)
    weighted = true_mask.astype(jnp.float32)[:, :, None]
    hidden_gap = final_rows - teacher_hidden.astype(jnp.float32)
    loss_part = jnp.sum(weighted * hidden_gap * hidden_gap)
    grad_final = 2.0 * weighted * hidden_gap
    pick_hot = (picked[:, :, None] == jnp.arange(seq_len)[None, None, :]).astype(jnp.bfloat16)
    chosen = (
        jnp.einsum(
            "spt,std->spd",
            pick_hot,
            final_rows.astype(jnp.bfloat16),
            preferred_element_type=jnp.float32,
        )
        .reshape(-1, row_width)
        .astype(jnp.bfloat16)
    )
    all_chosen = lax.all_to_all(
        jnp.broadcast_to(chosen[None], (n_dp,) + chosen.shape), SPLIT, split_axis=0, concat_axis=0
    ).reshape(n_dp * n_pick, row_width)
    slopes, chosen_part, head_loss = head_products(places, all_chosen, targets, tables)
    loss_part = loss_part + jnp.sum(head_loss)
    grad_chosen = lax.all_to_all(
        chosen_part.reshape(n_dp, n_pick, row_width), SPLIT, split_axis=0, concat_axis=0
    )
    order = [step for step in range(1, n_fs)] + [0]
    head_parts = [dense_tn(slopes[step], all_chosen) for step in order]
    grad_chosen, *head_parts = lax.optimization_barrier((grad_chosen, *head_parts))
    grad_chosen = jnp.sum(grad_chosen.astype(jnp.float32), axis=0)
    head_sum = head_parts[0]
    for part in head_parts[1:]:
        moved = lax.ppermute(head_sum.astype(jnp.bfloat16), "fsdp", ring)
        head_sum = moved.astype(jnp.float32) + part
    head_sum = head_sum[:own_rows]

    grad_hot = grad_chosen.reshape(seq_count, -1, row_width)
    grad_high = grad_hot.astype(jnp.bfloat16)
    grad_rest = (grad_hot - grad_high.astype(jnp.float32)).astype(jnp.bfloat16)
    for piece in (grad_high, grad_rest):
        grad_final = grad_final + jnp.einsum(
            "spt,spd->std", pick_hot, piece, preferred_element_type=jnp.float32
        )
    grad_layer = jnp.where(keep_rows, grad_final, 0.0)
    grad_inputs, matrix_grads, vector_grads = layer_backward(
        grad_layer.reshape(-1, row_width), lengths, matrices, vector_params, saved_state
    )
    grad_inputs = jnp.where(keep_rows, 0.0, grad_final) + grad_inputs.reshape(grad_final.shape)
    _, back_zero = jax.vjp(norm_rows, embedded, vector_params[0], vector_params[1])
    grad_embedded, gain_zero, shift_zero = back_zero(grad_inputs)
    grad_pos = jnp.sum(grad_embedded, axis=0)
    flat_grad = grad_embedded.reshape(-1, row_width)
    term_rows = send_rows(plan, 0, wanted, flat_grad, own_rows, axes)
    term_rows = more_sent(plan, rounds, term_rows, flat_grad, own_rows, axes)
    table_grad = head_sum + term_rows
    vector_all = jnp.concatenate([jnp.stack([gain_zero, shift_zero]), vector_grads])

    last = sum_to_owners(
        jnp.concatenate(
            [
                matrix_grads[0],
                grad_pos.T.astype(jnp.bfloat16),
                jnp.pad(vector_all.T, ((0, 0), (0, gain_width - 14))).astype(jnp.bfloat16),
            ],
            axis=1,
        )
    )
    out_grad, up_grad, down_grad = matrix_grads[1:]
    reduced = (
        last[:, 3 * row_width : 3 * row_width + seq_len].T,
        last[:, : 3 * row_width],
        out_grad,
        up_grad,
        down_grad,
        last[:, 3 * row_width + seq_len : 3 * row_width + seq_len + 14].T,
    )
    gradients = (table_grad,) + tuple(reduced)
    grad_squares = jnp.stack([jnp.sum(member * member) for member in gradients])
    weight_squares = jnp.stack([jnp.sum(member * member) for member in masters])
    totals = total_over(
        jnp.concatenate(
            [jnp.stack([loss_part, jnp.sum(weighted)]), grad_squares, weight_squares]
        ),
        axes,
    )
    loss_sum, token_count = totals[0], totals[1]
    grad_squares, weight_squares = totals[2:9], totals[9:16]
    grad_norm = jnp.sqrt(jnp.sum(grad_squares)) / token_count
    factor = jnp.minimum(1.0, CLIP_NORM / grad_norm) / token_count
    updates = []
    new_moments = []
    new_squares = []
    for weight, gradient, moment, square in zip(masters, gradients, firsts, seconds):
        clipped = gradient * factor
        moment_new = BETA_ONE * moment + (1.0 - BETA_ONE) * clipped
        square_new = BETA_TWO * square + (1.0 - BETA_TWO) * clipped * clipped
        updates.append(
            moment_new
            / (1.0 - BETA_ONE**STEP)
            / (jnp.sqrt(square_new / (1.0 - BETA_TWO**STEP)) + ADAM_EPS)
            + DECAY_RATE * weight
        )
        new_moments.append(moment_new)
        new_squares.append(square_new)
    update_squares = total_over(
        jnp.stack([jnp.sum(update * update) for update in updates]), axes
    )
    weight_norms = jnp.sqrt(weight_squares)
    update_norms = jnp.sqrt(update_squares)
    ratios = weight_norms / update_norms
    new_weights = [
        weight - LEARN_RATE * ratios[position] * update
        for position, (weight, update) in enumerate(zip(masters, updates))
    ]
    matrix_norms = jnp.stack([weight_norms, update_norms])
    return (
        loss_sum,
        token_count,
        grad_norm,
        new_weights[0],
        new_weights[1],
        new_weights[2],
        new_weights[3],
        new_weights[4],
        new_weights[5],
        new_weights[6],
        new_moments[0],
        new_moments[1],
        new_moments[2],
        new_moments[3],
        new_moments[4],
        new_moments[5],
        new_moments[6],
        new_squares[0],
        new_squares[1],
        new_squares[2],
        new_squares[3],
        new_squares[4],
        new_squares[5],
        new_squares[6],
        matrix_norms,
    )


def solution(mesh):
    split = Mesh(
        mesh.devices.reshape(mesh.shape["dp"] // 2, 2, mesh.shape["fsdp"]), AXES
    )
    placed = (
        P(AXES, None),
        P(AXES, None),
        P(AXES),
        P(AXES, None),
        P(AXES, None, None),
        P(AXES, None, None),
        P(AXES, None),
        P(None, AXES),
        P(AXES, None),
        P(AXES, None),
        P(AXES, None),
        P(AXES, None),
        P(None, AXES),
        P(AXES, None),
        P(None, AXES),
        P(AXES, None),
        P(AXES, None),
        P(AXES, None),
        P(AXES, None),
        P(None, AXES),
        P(AXES, None),
        P(None, AXES),
        P(AXES, None),
        P(AXES, None),
        P(AXES, None),
        P(AXES, None),
        P(None, AXES),
    )
    return jax.shard_map(
        on_device,
        mesh=split,
        in_specs=placed,
        out_specs=(
            P(),
            P(),
            P(),
            P(AXES, None),
            P(None, AXES),
            P(AXES, None),
            P(AXES, None),
            P(AXES, None),
            P(AXES, None),
            P(None, AXES),
            P(AXES, None),
            P(None, AXES),
            P(AXES, None),
            P(AXES, None),
            P(AXES, None),
            P(AXES, None),
            P(None, AXES),
            P(AXES, None),
            P(None, AXES),
            P(AXES, None),
            P(AXES, None),
            P(AXES, None),
            P(AXES, None),
            P(None, AXES),
            P(),
        ),
        check_vma=False,
    )
```

time: 5500 us -> 1010 us (0.18)
  blocking collectives: 4180 us -> 11.2 us
  local copies, waits for them, and re-layouts: 569 us -> 106 us
  waiting for transfers between devices: 152 us -> 331 us
  matrix products: 270 us -> 147 us
  starting transfers between devices: 13.2 us -> 135 us
  other arithmetic: 264 us -> 148 us
  Pallas kernels: 0 us -> 86.3 us
    unnamed x2 -> x0, blocking collectives: 3420 us -> none
    all_gather x2 -> x0, blocking collectives: 686 us -> none  [the longest x1 613 us: on_device(): lax.all_gather(lowered[6], ('dp', 'fsdp'), axis=1, tiled=True)]
    all_to_all x1 -> x15, waiting for transfers between devices: 0.01 us -> 279 us  [the longest x4 93.7 us: sum_to_owners(): part = lax.all_to_all(part, 'fsdp', split_axis=0, concat_axis=0)]
    unnamed x242 -> x198, local copies, waits for them, and re-layouts: 255 us -> 16.3 us
    reduce_scatter x5 -> x0, waiting for transfers between devices: 152 us -> none  [the longest x1 152 us: on_device(): lax.psum_scatter(dense(grad_logits, lowered[0]), ('dp', 'fsdp'), scatter_...]
    scatter-add x2 -> x0, other arithmetic: 144 us -> none  [the longest x1 131 us: on_device(): jax.ops.segment_sum(flat_grad, slot_ids, num_segments=count_rows + 1)]
    convert_element_type x9 -> x0, local copies, waits for them, and re-layouts: 111 us -> none  [the longest x2 90 us: on_device(): mismatch = logits - target_cols.reshape(logits.shape).astype(jnp.float32)]
    all_to_all x1 -> x15, starting transfers between devices: 7.3 us -> 115 us  [the longest x4 51.8 us: sum_to_owners(): part = lax.all_to_all(part, 'fsdp', split_axis=0, concat_axis=0)]
  transfers between devices with their start and end apart: 14 -> 26, of which waited for: 1 -> 16; matrix products, arithmetic and copies ran while one was open for 77% -> 23% of each run, Pallas kernels for 0% -> 4%
where the time goes in v1:
time: 1010 us; the launch traced here: 993 us
  waiting for transfers between devices  331 us (33%)
  other arithmetic  148 us (15%)
  matrix products  147 us (15%)
  starting transfers between devices  135 us (13%)
  local copies, waits for them, and re-layouts  106 us (10%)
  Pallas kernels  86.3 us (9%)
  between operations  27.4 us (3%)
  blocking collectives  11.2 us (1%)
    all_to_all x4, waiting for transfers between devices, sum_to_owners(): part = lax.all_to_all(part, 'fsdp', split_axis=0, concat_axis=0)  93.7 us
    all_to_all x1, waiting for transfers between devices, fetch_rows(): lax.all_to_all(rows.reshape(n_dev, room, -1), axes, split_axis=0, concat_...  75.8 us
    all_to_all x4, waiting for transfers between devices, sum_to_owners(): part = lax.all_to_all(part, 'plane', split_axis=0, concat_axis=0)  62.7 us
    dot_general x9, matrix products, dense(): return jnp.dot(left_op, right_op, preferred_element_type=jnp.float32)  57.9 us
    dot_general x8, matrix products, dense_tn(): lax.dot_general(left_op, right_op, (((0,), (0,)), ((), ())), preferred_el...  53.8 us
    all_to_all x4, starting transfers between devices, sum_to_owners(): part = lax.all_to_all(part, 'fsdp', split_axis=0, concat_axis=0)  51.8 us
    ppermute x3, waiting for transfers between devices, on_device(): tables.append(lax.ppermute(tables[-1], 'fsdp', ring))  51.1 us
    all_to_all x1, waiting for transfers between devices, send_rows(): lax.all_to_all(sums.reshape(n_dev, room, -1), axes, split_axis=0, concat_...  35.5 us
  transfers between devices with their start and end apart: 26, of which 16 were waited for; matrix products, arithmetic and copies ran while one was open for 23% of the time, Pallas kernels for 4%

profile of v1, /device:TPU:0, one launch (start us, length us, event | category | flops | bytes accessed | tf_op | source)
XLA Modules:
  0.0 993.3 jit_solution(10984494165416982598)
XLA Ops:
  24.0 7.3 all-to-all-start.4
  31.3 5.9 multiply_reduce_fusion.1
  38.6 5.2 fusion.51
  51.8 26.5 %shard_map.451 = bf16[32,128,1584]{2,1,0:T(8,128)(2,1)} custom-call(bf16[128,50304]{1,0:T(8,128)(2,1)} %bitcast.223), custom_call_target="tpu_custom_call" | custom-call | flops 25755648 | bytes 25755648 | tf_op jit(solution)/shard_map/pallas_call | solution.py:226
  78.4 17.9 %copy.134 = bf16[8,4,128,1584]{2,3,1,0:T(8,128)(2,1)} copy(bf16[8,4,128,1584]{3,2,1,0:T(8,128)(2,1)} %bitcast.218) | data formatting | bytes 25952256 | tf_op jit(solution)/shard_map/reshape | solution.py:582
  97.1 75.8 %all-to-all-done.5 = bf16[32,40,768]{2,1,0:T(8,128)(2,1)} async-done(((bf16[32,40,768]{2,1,0:T(8,128)(2,1)}), bf16[32,40,768]{2,1,0:T(8,128)(2,1)}, u32[]{:S(2)}, u32[]{:S(2)}) %all-to-all-start.5) | async-done | bytes 1966112 | tf_op jit(solution)/shard_map/all_to_all | solution.py:368
  178.6 18.1 %all-to-all-start.7 = ((bf16[8,4,128,1584]{2,3,1,0:T(8,128)(2,1)}), bf16[8,4,128,1584]{2,3,1,0:T(8,128)(2,1)}, u32[]{:S(2)}, u32[]{:S(2)}) async-start(bf16[8,4,128,1584]{2,3,1,0:T(8,128)(2,1)} %copy.134), calls=%async_computation.7 | async-start | bytes 25952256 | tf_op jit(solution)/shard_map/all_to_all | solution.py:581
  196.6 9.6 collective-permute-start.1
  208.0 51.1 %collective-permute-done.1.refs_2_ = bf16[1584,768]{1,0:T(8,128)(2,1)} collective-permute-done((bf16[1584,768]{1,0:T(8,128)(2,1)}, bf16[1584,768]{1,0:T(8,128)(2,1)}, u32[]{:S(2)}, u32[]{:S(2)}) %collective-permute-start.1) | collective-permute-done | bytes 2433056 | tf_op jit(solution)/shard_map/ppermute | solution.py:587
  274.7 4.8 slice.246
  279.6 8.6 reshape.670
  294.0 7.5 add_convert_fusion.1.query_ref.key_ref.value_ref
  301.5 11.9 %shard_map.450 = bf16[1024,768]{1,0:T(8,128)(2,1)} custom-call(s32[2]{0:T(128)} %broadcast_select_fusion.1.length_ref, bf16[1024,2304]{1,0:T(8,128)(2,1)} %add_convert_fusion.1.query_ref.key_ref.value_ref, bf16[1024,2304]{1,0:T(8,128)(2,1)} %add_convert_fusion.1.query_ref.key_ref.value_ref, bf16[1024,2304]{1,0:T(8,128)(2,1)} %add_convert_fusion.1.query_ref.key_ref.value_ref), custom_call_target="tpu_custom_call" | custom-call | flops 6442450944 | bytes 6291456 | tf_op jit(solution)/shard_map/pallas_call | solution.py:174
  318.2 12.2 %multiply_convert_fusion = (bf16[1024,3072]{1,0:T(8,128)(2,1)S(1)}, f32[1024,3072]{1,0:T(8,128)}) fusion(f32[3072]{0:T(1024)S(1)} %copy-done.80, bf16[768,9856]{1,0:T(8,128)(2,1)} %all-gather.2.cloned.1.call-done, f32[1024,768]{1,0:T(8,128)S(1)} %get-tuple-element.573, f32[768]{0:T(1024)S(1)} %get-tuple-element.454, f32[768]{0:T(1024)S(1)} %get-tuple-element.455, ...), kind=kOutput, calls=%fused_computation.35 | convolution fusion | flops 4854644736 | bytes 26765312 | tf_op jit(solution)/shard_map/dot_general | solution.py:47
  330.5 5.4 fusion.121
  348.2 17.8 %copy.135.target_ref = bf16[8,4,128,1584]{3,2,1,0:T(8,128)(2,1)} copy(bf16[8,4,128,1584]{2,3,1,0:T(8,128)(2,1)} %all-to-all-done.7) | data formatting | bytes 25952256 | tf_op jit(solution)/shard_map/all_to_all | solution.py:581
  369.2 33.1 %shard_map.452 = (bf16[4,1024,1584]{2,1,0:T(8,128)(2,1)}, bf16[1024,768]{1,0:T(8,128)(2,1)}, f32[8,1584]{1,0:T(8,128)}) custom-call(s32[4]{0:T(128)} %compare_select_fusion.place_ref, bf16[1024,768]{1,0:T(8,128)(2,1)} %bitcast.243, bf16[8,4,128,1584]{3,2,1,0:T(8,128)(2,1)} %copy.135.target_ref, bf16[1584,768]{1,0:T(8,128)(2,1)} %pad.33.refs_0_, ...), custom_call_target="tpu_custom_call" | custom-call | flops 19931332608 | bytes 35684352 | tf_op jit(solution)/shard_map/pallas_call | solution.py:273
  402.3 6.6 fusion.45
  413.5 6.9 fusion.43
  420.5 7.0 fusion.41
  427.4 6.9 fusion.39
  443.9 7.0 convolution_convert_fusion.1
  450.9 11.8 %fusion.122 = (bf16[3072]{0:T(1024)(128)(2,1)S(1)}, bf16[1024,3072]{1,0:T(8,128)(2,1)S(1)}) fusion(f32[1024,3072]{1,0:T(8,128)} %get-tuple-element.575, f32[3072]{0:T(1024)S(1)} %copy-done.80, bf16[1024,768]{1,0:T(8,128)(2,1)S(1)} %get-tuple-element.529, bf16[3072,768]{1,0:T(8,128)(2,1)S(1)} %bitcast.232), kind=kOutput, calls=%fused_computation.298 | convolution fusion | flops 4869583872 | bytes 25184256 | tf_op jit(solution)/shard_map/dot_general | solution.py:57
  462.7 8.3 convolution_convert_fusion
  471.0 8.4 multiply_reduce_fusion.3
  489.8 14.8 %shard_map.453 = (bf16[1024,768]{1,0:T(8,128)(2,1)}, bf16[1024,768]{1,0:T(8,128)(2,1)}, bf16[1024,768]{1,0:T(8,128)(2,1)}) custom-call(s32[2]{0:T(128)} %broadcast_select_fusion.1.length_ref, bf16[1024,2304]{1,0:T(8,128)(2,1)} %add_convert_fusion.1.query_ref.key_ref.value_ref, bf16[1024,2304]{1,0:T(8,128)(2,1)} %add_convert_fusion.1.query_ref.key_ref.value_ref, ...), custom_call_target="tpu_custom_call" | custom-call | flops 16106127360 | bytes 11010048 | tf_op jit(solution)/shard_map/pallas_call | solution.py:174
  513.0 8.6 convolution_convert_fusion.2
  521.7 7.0 add_add_fusion.6
  535.0 5.0 fusion.108
  542.7 6.3 fusion.22
  554.3 6.4 add_convert_fusion.4
  565.8 40.3 %all-to-all-start.13 = ((bf16[4,24,768]{2,1,0:T(8,128)(2,1)}), bf16[4,24,768]{2,1,0:T(8,128)(2,1)S(1)}, u32[]{:S(2)}, u32[]{:S(2)}) async-start(bf16[4,24,768]{2,1,0:T(8,128)(2,1)} %bitcast.48), calls=%async_computation.13 | async-start | bytes 294912 | tf_op jit(solution)/shard_map/all_to_all | solution.py:315
  624.8 35.5 %all-to-all-done.9 = bf16[32,40,768]{2,1,0:T(8,128)(2,1)} async-done(((bf16[32,40,768]{2,1,0:T(8,128)(2,1)}), bf16[32,40,768]{2,1,0:T(8,128)(2,1)}, u32[]{:S(2)}, u32[]{:S(2)}) %all-to-all-start.9) | async-done | bytes 1966112 | tf_op jit(solution)/shard_map/all_to_all | solution.py:392
  671.3 4.7 fusion.28
  676.0 16.5 %all-to-all-done.10 = bf16[4,96,2944]{2,1,0:T(8,128)(2,1)} async-done(((bf16[4,96,2944]{2,1,0:T(8,128)(2,1)}), bf16[4,96,2944]{2,1,0:T(8,128)(2,1)}, u32[]{:S(2)}, u32[]{:S(2)}) %all-to-all-start.10) | async-done | bytes 2261024 | tf_op jit(solution)/shard_map/all_to_all | solution.py:312
  701.3 24.3 %all-to-all-done.14 = bf16[4,96,3072]{2,1,0:T(8,128)(2,1)} async-done(((bf16[4,96,3072]{2,1,0:T(8,128)(2,1)}), bf16[4,96,3072]{2,1,0:T(8,128)(2,1)}, u32[]{:S(2)}, u32[]{:S(2)}) %all-to-all-start.14) | async-done | bytes 2359328 | tf_op jit(solution)/shard_map/all_to_all | solution.py:312
  730.2 5.1 add_convert_fusion.3
  739.3 18.7 %all-to-all-done.16 = bf16[4,384,768]{2,1,0:T(8,128)(2,1)} async-done(((bf16[4,384,768]{2,1,0:T(8,128)(2,1)}), bf16[4,384,768]{2,1,0:T(8,128)(2,1)}, u32[]{:S(2)}, u32[]{:S(2)}) %all-to-all-start.16) | async-done | bytes 2359328 | tf_op jit(solution)/shard_map/all_to_all | solution.py:312
  777.0 27.0 %all-to-all-done.11 = bf16[4,24,2944]{2,1,0:T(8,128)(2,1)} async-done(((bf16[4,24,2944]{2,1,0:T(8,128)(2,1)}), bf16[4,24,2944]{2,1,0:T(8,128)(2,1)}, u32[]{:S(2)}, u32[]{:S(2)}) %all-to-all-start.11) | async-done | bytes 565280 | tf_op jit(solution)/shard_map/all_to_all | solution.py:315
  807.9 6.7 fusion.21
  827.8 5.1 add_convert_fusion.2
  835.6 59.7 %all-to-all-done.17 = bf16[4,96,768]{2,1,0:T(8,128)(2,1)S(1)} async-done(((bf16[4,96,768]{2,1,0:T(8,128)(2,1)}), bf16[4,96,768]{2,1,0:T(8,128)(2,1)S(1)}, u32[]{:S(2)}, u32[]{:S(2)}) %all-to-all-start.17) | async-done | bytes 589856 | tf_op jit(solution)/shard_map/all_to_all | solution.py:315
  897.0 8.7 multiply_reduce_fusion.2
  905.7 9.7 concatenate.39
  915.5 11.2 %all_to_all.116 = f32[32,8,128]{2,1,0:T(8,128)S(1)} all-to-all(f32[32,8,128]{2,1,0:T(8,128)S(1)} %broadcast_in_dim.214), channel_id=1, replica_groups=mesh['plane'=4,'pair'=2,'fsdp'=4] {'plane','pair','fsdp'}, dimensions={0} | all-to-all | bytes 262144 | tf_op jit(solution)/shard_map/all_to_all | solution.py:322
  938.6 9.8 multiply_reduce_fusion
  957.0 7.7 all-to-all-done.19
  970.5 10.0 %multiply_subtract_fusion = f32[1572,768]{1,0:T(8,128)} fusion(f32[1572,768]{1,0:T(8,128)} %param.41, f32[]{:T(128)} %bitcast.83, f32[1572,768]{1,0:T(8,128)} %get-tuple-element.523, f32[1572,768]{1,0:T(8,128)} %get-tuple-element.522), kind=kLoop, calls=%fused_computation.59 | loop fusion | flops 9658368 | bytes 19316740 | tf_op jit(solution)/shard_map/sub | solution.py:704
  (391 shorter events, 235.3 us)
Async XLA Ops:
  7.2 254.4 %all-gather.2.cloned.1.call-start = ((), (), s32[]{:S(2)}) async-start(), calls=%async_computation.20 | async-start | bytes 15611904 | tf_op jit(solution)/shard_map/all_gather | solution.py:565
  22.5 150.4 %copy-start.75 = (s32[1024]{0:T(1024)}, s32[1024]{0:T(1024)S(1)}, u32[]{:S(2)}) copy-start(s32[1024]{0:T(1024)S(1)} %add_select_fusion.5) | copy-start | bytes 12292
  24.0 14.6 %all-to-all-start.4 = ((s32[32,1,128]{2,1,0:T(1,128)}), s32[32,1,128]{2,1,0:T(1,128)S(1)}, u32[]{:S(2)}, u32[]{:S(2)}) async-start(s32[32,1,128]{2,1,0:T(1,128)} %bitcast.8), calls=%async_computation.4 | async-start | bytes 32768 | tf_op jit(solution)/shard_map/all_to_all | solution.py:360
  43.9 129.0 %all-to-all-start.5 = ((bf16[32,40,768]{2,1,0:T(8,128)(2,1)}), bf16[32,40,768]{2,1,0:T(8,128)(2,1)}, u32[]{:S(2)}, u32[]{:S(2)}) async-start(bf16[32,40,768]{2,1,0:T(8,128)(2,1)} %bitcast.239), calls=%async_computation.5 | async-start | bytes 3932160 | tf_op jit(solution)/shard_map/all_to_all | solution.py:368
  50.1 146.5 %collective-permute-start = (bf16[1584,768]{1,0:T(8,128)(2,1)}, bf16[1584,768]{1,0:T(8,128)(2,1)}, u32[]{:S(2)}, u32[]{:S(2)}) collective-permute-start(bf16[1584,768]{1,0:T(8,128)(2,1)} %pad.33.refs_0_), channel_id=1, source_target_pairs={{0,1},{1,2},{2,3},{3,0},{4,5},{5,6},{6,7},{7,4},{8,9},{9,10},{10,1... | collective-permute-start | bytes 7299080 | tf_op jit(solution)/shard_map/ppermute | solution.py:587
  178.0 159.6 %copy-start = (f32[1024,768]{1,0:T(8,128)}, f32[1024,768]{1,0:T(8,128)S(1)}, u32[]{:S(2)}) copy-start(f32[1024,768]{1,0:T(8,128)S(1)} %get-tuple-element.326) | copy-start | bytes 9437188
  178.6 162.8 %all-to-all-start.7 = ((bf16[8,4,128,1584]{2,3,1,0:T(8,128)(2,1)}), bf16[8,4,128,1584]{2,3,1,0:T(8,128)(2,1)}, u32[]{:S(2)}, u32[]{:S(2)}) async-start(bf16[8,4,128,1584]{2,3,1,0:T(8,128)(2,1)} %copy.134), calls=%async_computation.7 | async-start | bytes 25952256 | tf_op jit(solution)/shard_map/all_to_all | solution.py:581
  196.6 62.5 %collective-permute-start.1 = (bf16[1584,768]{1,0:T(8,128)(2,1)}, bf16[1584,768]{1,0:T(8,128)(2,1)}, u32[]{:S(2)}, u32[]{:S(2)}) collective-permute-start(bf16[1584,768]{1,0:T(8,128)(2,1)} %collective-permute-done.refs_1_), channel_id=1, source_target_pairs={{0,1},{1,2},{2,3},{3,0},{4,5},{5,6},{6,7},{7,4},{8,9},{9,10},{10,1... | collective-permute-start | bytes 7299080 | tf_op jit(solution)/shard_map/ppermute | solution.py:587
  259.1 106.8 %collective-permute-start.2 = (bf16[1584,768]{1,0:T(8,128)(2,1)}, bf16[1584,768]{1,0:T(8,128)(2,1)}, u32[]{:S(2)}, u32[]{:S(2)}) collective-permute-start(bf16[1584,768]{1,0:T(8,128)(2,1)} %collective-permute-done.1.refs_2_), channel_id=1, source_target_pairs={{0,1},{1,2},{2,3},{3,0},{4,5},{5,6},{6,7},{7,4},{8,9},{9,10},{10,1... | collective-permute-start | bytes 7299080 | tf_op jit(solution)/shard_map/ppermute | solution.py:587
  269.8 67.8 %copy-start.63 = (f32[2,512]{1,0:T(2,128)}, f32[2,512]{1,0:T(2,128)S(1)}, u32[]{:S(2)}) copy-start(f32[2,512]{1,0:T(2,128)S(1)} %div.214) | copy-start | bytes 12292
  290.1 47.5 %copy-start.65 = (f32[2,512]{1,0:T(2,128)}, f32[2,512]{1,0:T(2,128)S(1)}, u32[]{:S(2)}) copy-start(f32[2,512]{1,0:T(2,128)S(1)} %rsqrt.41) | copy-start | bytes 12292
  292.1 45.5 %copy-start.57 = (f32[768]{0:T(1024)}, f32[768]{0:T(1024)S(1)}, u32[]{:S(2)}) copy-start(f32[768]{0:T(1024)S(1)} %get-tuple-element.460) | copy-start | bytes 9220
  342.7 25.3 %all-to-all-start.6 = ((bf16[8,128,768]{2,1,0:T(8,128)(2,1)}), bf16[8,128,768]{2,1,0:T(8,128)(2,1)S(1)}, u32[]{:S(2)}, u32[]{:S(2)}) async-start(bf16[8,128,768]{2,1,0:T(8,128)(2,1)} %broadcast_in_dim.204), calls=%async_computation.6 | async-start | bytes 3145728 | tf_op jit(solution)/shard_map/all_to_all | solution.py:611
  408.9 25.7 %all-to-all-start.8 = ((bf16[8,128,768]{2,1,0:T(8,128)(2,1)}), bf16[8,128,768]{2,1,0:T(8,128)(2,1)}, u32[]{:S(2)}, u32[]{:S(2)}) async-start(bf16[8,128,768]{2,1,0:T(8,128)(2,1)} %bitcast.25), calls=%async_computation.8 | async-start | bytes 3145728 | tf_op jit(solution)/shard_map/all_to_all | solution.py:616
  542.2 6.8 collective-permute-start.7
  550.0 14.0 %all-to-all-start.12 = ((bf16[4,96,768]{2,1,0:T(8,128)(2,1)}), bf16[4,96,768]{2,1,0:T(8,128)(2,1)}, u32[]{:S(2)}, u32[]{:S(2)}) async-start(bf16[4,96,768]{2,1,0:T(8,128)(2,1)} %fusion.70), calls=%async_computation.12 | async-start | bytes 1179648 | tf_op jit(solution)/shard_map/all_to_all | solution.py:312
  565.8 46.5 %all-to-all-start.13 = ((bf16[4,24,768]{2,1,0:T(8,128)(2,1)}), bf16[4,24,768]{2,1,0:T(8,128)(2,1)S(1)}, u32[]{:S(2)}, u32[]{:S(2)}) async-start(bf16[4,24,768]{2,1,0:T(8,128)(2,1)} %bitcast.48), calls=%async_computation.13 | async-start | bytes 294912 | tf_op jit(solution)/shard_map/all_to_all | solution.py:315
  612.3 47.9 %all-to-all-start.9 = ((bf16[32,40,768]{2,1,0:T(8,128)(2,1)}), bf16[32,40,768]{2,1,0:T(8,128)(2,1)}, u32[]{:S(2)}, u32[]{:S(2)}) async-start(bf16[32,40,768]{2,1,0:T(8,128)(2,1)} %bitcast.238), calls=%async_computation.9 | async-start | bytes 3932160 | tf_op jit(solution)/shard_map/all_to_all | solution.py:392
  618.4 4.5 collective-permute-start.6
  621.8 49.6 %collective-permute-start.8 = (bf16[4,96,3072]{2,1,0:T(8,128)(2,1)}, bf16[4,96,3072]{2,1,0:T(8,128)(2,1)}, u32[]{:S(2)}, u32[]{:S(2)}) collective-permute-start(bf16[4,96,3072]{2,1,0:T(8,128)(2,1)} %dynamic-slice_bitcast_fusion.1), channel_id=1, source_target_pairs={{0,4},{4,0},{1,5},{5,1},{2,6},{6,2},{3,7},{7,3},{8,12},{12,8},{9,1... | collective-permute-start | bytes 7077896 | tf_op jit(solution)/shard_map/ppermute | solution.py:310
  660.3 32.2 %all-to-all-start.10 = ((bf16[4,96,2944]{2,1,0:T(8,128)(2,1)}), bf16[4,96,2944]{2,1,0:T(8,128)(2,1)}, u32[]{:S(2)}, u32[]{:S(2)}) async-start(bf16[4,96,2944]{2,1,0:T(8,128)(2,1)} %fusion.30), calls=%async_computation.10 | async-start | bytes 4521984 | tf_op jit(solution)/shard_map/all_to_all | solution.py:312
  668.0 29.0 %collective-permute-start.9 = (bf16[4,384,768]{2,1,0:T(8,128)(2,1)}, bf16[4,384,768]{2,1,0:T(8,128)(2,1)}, u32[]{:S(2)}, u32[]{:S(2)}) collective-permute-start(bf16[4,384,768]{2,1,0:T(8,128)(2,1)} %dynamic-slice_bitcast_fusion), channel_id=1, source_target_pairs={{0,4},{4,0},{1,5},{5,1},{2,6},{6,2},{3,7},{7,3},{8,12},{12,8},{9,1... | collective-permute-start | bytes 7077896 | tf_op jit(solution)/shard_map/ppermute | solution.py:310
  669.3 60.9 %collective-permute-start.3 = (bf16[1584,768]{1,0:T(8,128)(2,1)}, bf16[1584,768]{1,0:T(8,128)(2,1)}, u32[]{:S(2)}, u32[]{:S(2)}) collective-permute-start(bf16[1584,768]{1,0:T(8,128)(2,1)} %fusion.45), channel_id=1, source_target_pairs={{0,1},{1,2},{2,3},{3,0},{4,5},{5,6},{6,7},{7,4},{8,9},{9,10},{10,1... | collective-permute-start | bytes 7299080 | tf_op jit(solution)/shard_map/ppermute | solution.py:625
  692.5 33.2 %all-to-all-start.14 = ((bf16[4,96,3072]{2,1,0:T(8,128)(2,1)}), bf16[4,96,3072]{2,1,0:T(8,128)(2,1)}, u32[]{:S(2)}, u32[]{:S(2)}) async-start(bf16[4,96,3072]{2,1,0:T(8,128)(2,1)} %fusion.28), calls=%async_computation.14 | async-start | bytes 4718592 | tf_op jit(solution)/shard_map/all_to_all | solution.py:312
  725.6 32.4 %all-to-all-start.16 = ((bf16[4,384,768]{2,1,0:T(8,128)(2,1)}), bf16[4,384,768]{2,1,0:T(8,128)(2,1)}, u32[]{:S(2)}, u32[]{:S(2)}) async-start(bf16[4,384,768]{2,1,0:T(8,128)(2,1)} %fusion.27), calls=%async_computation.16 | async-start | bytes 4718592 | tf_op jit(solution)/shard_map/all_to_all | solution.py:312
  735.3 92.4 %collective-permute-start.4 = (bf16[1584,768]{1,0:T(8,128)(2,1)}, bf16[1584,768]{1,0:T(8,128)(2,1)}, u32[]{:S(2)}, u32[]{:S(2)}) collective-permute-start(bf16[1584,768]{1,0:T(8,128)(2,1)} %add_convert_fusion.3), channel_id=1, source_target_pairs={{0,1},{1,2},{2,3},{3,0},{4,5},{5,6},{6,7},{7,4},{8,9},{9,10},{10,1... | collective-permute-start | bytes 7299080 | tf_op jit(solution)/shard_map/ppermute | solution.py:625
  758.1 45.9 %all-to-all-start.11 = ((bf16[4,24,2944]{2,1,0:T(8,128)(2,1)}), bf16[4,24,2944]{2,1,0:T(8,128)(2,1)}, u32[]{:S(2)}, u32[]{:S(2)}) async-start(bf16[4,24,2944]{2,1,0:T(8,128)(2,1)} %bitcast.237), calls=%async_computation.11 | async-start | bytes 1130496 | tf_op jit(solution)/shard_map/all_to_all | solution.py:315
  769.0 38.9 %copy-start.85 = (s32[1280]{0:T(1024)S(1)}, s32[1280]{0:T(1024)}, u32[]{:S(2)}) copy-start(s32[1280]{0:T(1024)} %copy-done.84) | copy-start | bytes 15364
  804.0 20.2 %all-to-all-start.15 = ((bf16[4,24,3072]{2,1,0:T(8,128)(2,1)}), bf16[4,24,3072]{2,1,0:T(8,128)(2,1)S(1)}, u32[]{:S(2)}, u32[]{:S(2)}) async-start(bf16[4,24,3072]{2,1,0:T(8,128)(2,1)} %bitcast.53), calls=%async_computation.15 | async-start | bytes 1179648 | tf_op jit(solution)/shard_map/all_to_all | solution.py:315
  824.2 71.1 %all-to-all-start.17 = ((bf16[4,96,768]{2,1,0:T(8,128)(2,1)}), bf16[4,96,768]{2,1,0:T(8,128)(2,1)S(1)}, u32[]{:S(2)}, u32[]{:S(2)}) async-start(bf16[4,96,768]{2,1,0:T(8,128)(2,1)} %bitcast.58), calls=%async_computation.17 | async-start | bytes 1179648 | tf_op jit(solution)/shard_map/all_to_all | solution.py:315
  827.7 68.4 %copy-start.40 = (s32[1024]{0:T(1024)S(1)}, s32[1024]{0:T(1024)}, u32[]{:S(2)}) copy-start(s32[1024]{0:T(1024)} %copy-done.39) | copy-start | bytes 12292
  827.7 68.4 %copy-start.45 = (s32[1024]{0:T(1024)S(1)}, s32[1024]{0:T(1024)}, u32[]{:S(2)}) copy-start(s32[1024]{0:T(1024)} %copy-done.44) | copy-start | bytes 12292
  827.7 68.4 %copy-start.47 = (s32[1024]{0:T(1024)S(1)}, s32[1024]{0:T(1024)}, u32[]{:S(2)}) copy-start(s32[1024]{0:T(1024)} %copy-done.46) | copy-start | bytes 12292
  827.7 68.4 %copy-start.56 = (pred[1024]{0:T(1024)(128)(4,1)S(1)}, pred[1024]{0:T(1024)(128)(4,1)}, u32[]{:S(2)}) copy-start(pred[1024]{0:T(1024)(128)(4,1)} %copy-done.55) | copy-start | bytes 3076
  827.7 68.3 %copy-start.60 = (pred[1024]{0:T(1024)(128)(4,1)S(1)}, pred[1024]{0:T(1024)(128)(4,1)}, u32[]{:S(2)}) copy-start(pred[1024]{0:T(1024)(128)(4,1)} %copy-done.59) | copy-start | bytes 3076
  832.9 64.0 %collective-permute-start.5 = (bf16[1584,768]{1,0:T(8,128)(2,1)}, bf16[1584,768]{1,0:T(8,128)(2,1)}, u32[]{:S(2)}, u32[]{:S(2)}) collective-permute-start(bf16[1584,768]{1,0:T(8,128)(2,1)} %add_convert_fusion.2), channel_id=1, source_target_pairs={{0,1},{1,2},{2,3},{3,0},{4,5},{5,6},{6,7},{7,4},{8,9},{9,10},{10,1... | collective-permute-start | bytes 7299080 | tf_op jit(solution)/shard_map/ppermute | solution.py:625
  931.3 49.3 %copy-start.53 = (f32[512,24]{0,1:T(8,128)}, f32[512,24]{0,1:T(8,128)S(1)}, u32[]{:S(2)}) copy-start(f32[512,24]{0,1:T(8,128)S(1)} %get-tuple-element.519) | copy-start | bytes 147460
  933.2 48.0 %copy-start.35 = (f32[24,2304]{1,0:T(8,128)}, f32[24,2304]{1,0:T(8,128)S(1)}, u32[]{:S(2)}) copy-start(f32[24,2304]{1,0:T(8,128)S(1)} %get-tuple-element.516) | copy-start | bytes 663556
  933.2 48.0 %copy-start.36 = (f32[24,2304]{1,0:T(8,128)}, f32[24,2304]{1,0:T(8,128)S(1)}, u32[]{:S(2)}) copy-start(f32[24,2304]{1,0:T(8,128)S(1)} %get-tuple-element.517) | copy-start | bytes 663556
  934.9 47.2 %copy-start.48 = (f32[24,768]{1,0:T(8,128)}, f32[24,768]{1,0:T(8,128)S(1)}, u32[]{:S(2)}) copy-start(f32[24,768]{1,0:T(8,128)S(1)} %get-tuple-element.513) | copy-start | bytes 221188
  934.9 47.2 %copy-start.49 = (f32[24,768]{1,0:T(8,128)}, f32[24,768]{1,0:T(8,128)S(1)}, u32[]{:S(2)}) copy-start(f32[24,768]{1,0:T(8,128)S(1)} %get-tuple-element.514) | copy-start | bytes 221188
  935.7 47.0 %copy-start.31 = (f32[24,3072]{1,0:T(8,128)}, f32[24,3072]{1,0:T(8,128)S(1)}, u32[]{:S(2)}) copy-start(f32[24,3072]{1,0:T(8,128)S(1)} %get-tuple-element.510) | copy-start | bytes 884740
  935.7 47.0 %copy-start.32 = (f32[24,3072]{1,0:T(8,128)}, f32[24,3072]{1,0:T(8,128)S(1)}, u32[]{:S(2)}) copy-start(f32[24,3072]{1,0:T(8,128)S(1)} %get-tuple-element.511) | copy-start | bytes 884740
  937.9 45.8 %copy-start.33 = (f32[96,768]{1,0:T(8,128)}, f32[96,768]{1,0:T(8,128)S(1)}, u32[]{:S(2)}) copy-start(f32[96,768]{1,0:T(8,128)S(1)} %get-tuple-element.507) | copy-start | bytes 884740
  937.9 45.8 %copy-start.34 = (f32[96,768]{1,0:T(8,128)}, f32[96,768]{1,0:T(8,128)S(1)}, u32[]{:S(2)}) copy-start(f32[96,768]{1,0:T(8,128)S(1)} %get-tuple-element.508) | copy-start | bytes 884740
  938.6 46.0 %copy-start.73 = (f32[14,24]{1,0:T(8,128)}, f32[14,24]{1,0:T(8,128)S(1)}, u32[]{:S(2)}) copy-start(f32[14,24]{1,0:T(8,128)S(1)} %get-tuple-element.504) | copy-start | bytes 4036
  938.6 46.0 %copy-start.74 = (f32[14,24]{1,0:T(8,128)}, f32[14,24]{1,0:T(8,128)S(1)}, u32[]{:S(2)}) copy-start(f32[14,24]{1,0:T(8,128)S(1)} %get-tuple-element.505) | copy-start | bytes 4036
  953.7 11.0 %all-to-all-start.19 = ((f32[32,8,128]{2,1,0:T(8,128)}), f32[32,8,128]{2,1,0:T(8,128)S(1)}, u32[]{:S(2)}, u32[]{:S(2)}) async-start(f32[32,8,128]{2,1,0:T(8,128)} %broadcast_in_dim.217), calls=%async_computation.19 | async-start | bytes 262144 | tf_op jit(solution)/shard_map/all_to_all | solution.py:322
  (74 other events, 898.8 us)
Sparse Core Ops, SparseCore 0:
  15.1 244.4 all-gather.1
